TPU v7x, 256 devices: a whole 4x4x8 slice. The times are simulated.
256 devices in a mesh: ctx: 64 (over y, z, core), tp: 4 (over x).
Axes of the slice: x: 4, y: 4, z: 8, core: 2. Of those that a mesh axis runs over, the one named last changes fastest.
Arguments:
- queries: bfloat16 [32768, 4096], P(('ctx', 'tp')), may hold values from -6 to 6
- key_states: bfloat16 [32768, 512], P(('ctx', 'tp')), may hold values from -6 to 6
- value_projection: bfloat16 [32768, 512], P(('ctx', 'tp')), may hold values from -6 to 6
- output_gradient: bfloat16 [32768, 4096], P(('ctx', 'tp')), may hold values from -6 to 6
- doc_ids: int32 [32768], replicated, may hold values from 0 to 127, never falling along the last dimension, each value on 1 to 1536 neighbouring positions
- pair_live: int32 [64, 4], P('ctx'), may hold values from 0 to 1, as said below
Outputs:
- attention: bfloat16 [32768, 4096], P('ctx', 'tp')
- query_grad: bfloat16 [32768, 4096], P('ctx', 'tp')
- key_grad: bfloat16 [32768, 512], P('ctx', 'tp')
- value_grad: bfloat16 [32768, 512], P('ctx', 'tp')
Inputs may be any that keep to these rules, and one draw needn't show every extreme that they name: `pair_live`: entry [b, 0] is 1; entry [b, r] is 0 where r > b.
All inputs are finite; a program needn't handle non-finite values.
Results may differ from a plain program's by a relative error of at most 0.02.
Values may be sent and summed in bfloat16 or wider, within the bound.
No kernel may reach another device: no remote copies, remote signals or barrier semaphores. Data moves between devices by JAX's collectives and lax.ppermute only.
A program may use at most 64 MiB of HBM per device.

v0:
```python
import jax
import jax.numpy as jnp
from jax import lax
from jax.sharding import PartitionSpec as P

HEAD_SIZE = 128
HEADS_PER_GROUP = 8
PAIRS = 4


def passed_along(value, axis, steps):
    count = lax.axis_size(axis)
    initial, last = (max(0, -steps), min(count, count - steps))
    return lax.ppermute(value, axis, [(source, source + steps) for source in range(initial, last)])


def build_mask(doc_ids, pair_row, blk_index, rows_per_block):
    positions = jnp.arange(rows_per_block, dtype=jnp.int32)
    query_start = blk_index * rows_per_block
    query_ids = lax.dynamic_slice_in_dim(doc_ids, query_start, rows_per_block)
    mask_list = []
    for offset in range(PAIRS):
        key_block = blk_index - offset
        key_start = jnp.maximum(key_block, 0) * rows_per_block
        key_ids = lax.dynamic_slice_in_dim(doc_ids, key_start, rows_per_block)
        same_doc = query_ids[:, None] == key_ids[None, :]
        causal = (key_block * rows_per_block + positions)[None, :] <= (query_start + positions)[
            :, None
        ]
        live_pair = (pair_row[offset] == 1) & (key_block >= 0)
        mask_list.append(same_doc & causal & live_pair)
    return jnp.concatenate(mask_list, axis=1)


def attend(query_grp, grad_grp, key_grp, value_grp, allowed, scaling):
    query_seq = jnp.transpose(query_grp, (1, 0, 2))
    grad_seq = jnp.transpose(grad_grp, (1, 0, 2))

    def one_head(totals, inputs):
        query_one, grad_one = inputs
        scores = jnp.dot(query_one, key_grp.T, preferred_element_type=jnp.float32) * scaling
        scores = jnp.where(allowed, scores, -1e30)
        row_max = jnp.max(scores, axis=1, keepdims=True)
        exponent = jnp.exp(scores - row_max)
        attn_probs = exponent / jnp.sum(exponent, axis=1, keepdims=True)
        probs_low = attn_probs.astype(jnp.bfloat16)
        output = jnp.dot(probs_low, value_grp, preferred_element_type=jnp.float32).astype(
            jnp.bfloat16
        )
        prob_grad = jnp.dot(grad_one, value_grp.T, preferred_element_type=jnp.float32)
        row_delta = jnp.sum(
            grad_one.astype(jnp.float32) * output.astype(jnp.float32), axis=1, keepdims=True
        )
        score_grad = (attn_probs * (prob_grad - row_delta)).astype(jnp.bfloat16)
        query_grad = (
            jnp.dot(score_grad, key_grp, preferred_element_type=jnp.float32) * scaling
        ).astype(jnp.bfloat16)
        key_part = jnp.dot(score_grad.T, query_one, preferred_element_type=jnp.float32) * scaling
        value_part = jnp.dot(probs_low.T, grad_one, preferred_element_type=jnp.float32)
        return ((totals[0] + key_part, totals[1] + value_part), (output, query_grad))

    empty = jnp.zeros((key_grp.shape[0], key_grp.shape[1]), jnp.float32)
    (key_total, value_total), (outputs, query_grads) = lax.scan(
        one_head, (empty, empty), (query_seq, grad_seq)
    )
    return (
        jnp.transpose(outputs, (1, 0, 2)),
        jnp.transpose(query_grads, (1, 0, 2)),
        key_total,
        value_total,
    )


def local(queries, key_states, value_projection, output_gradient, doc_ids, pair_live):
    query_heads, key_heads, value_heads, grad_heads = (
        lax.all_to_all(queries, "tp", split_axis=1, concat_axis=0, tiled=True),
        lax.all_to_all(key_states, "tp", split_axis=1, concat_axis=0, tiled=True),
        lax.all_to_all(value_projection, "tp", split_axis=1, concat_axis=0, tiled=True),
        lax.all_to_all(output_gradient, "tp", split_axis=1, concat_axis=0, tiled=True),
    )
    rows_per_block = query_heads.shape[0]
    key_value_width = key_heads.shape[1]
    scaling = HEAD_SIZE ** (-0.5)
    blk_index = lax.axis_index("ctx")
    joined = jnp.concatenate([key_heads, value_heads], axis=1)
    arrived = [joined]
    for offset in range(1, PAIRS):
        arrived.append(passed_along(joined, "ctx", offset))
    resident = jnp.concatenate(arrived, axis=0)
    allowed = build_mask(doc_ids, pair_live[0], blk_index, rows_per_block)
    query_grp = query_heads.reshape(rows_per_block, HEADS_PER_GROUP, HEAD_SIZE)
    grad_grp = grad_heads.reshape(rows_per_block, HEADS_PER_GROUP, HEAD_SIZE)
    key_grp = resident[:, 0:HEAD_SIZE]
    value_grp = resident[:, key_value_width : key_value_width + HEAD_SIZE]
    output, query_grad, key_part, value_part = attend(
        query_grp, grad_grp, key_grp, value_grp, allowed, scaling
    )
    out_list = [output]
    qgrad_list = [query_grad]
    kgrad_list = [key_part]
    vgrad_list = [value_part]
    attention = jnp.stack(out_list, axis=1).reshape(rows_per_block, -1)
    query_grad = jnp.stack(qgrad_list, axis=1).reshape(rows_per_block, -1)
    key_all = jnp.stack(kgrad_list, axis=1).reshape(PAIRS * rows_per_block, key_value_width)
    value_all = jnp.stack(vgrad_list, axis=1).reshape(PAIRS * rows_per_block, key_value_width)
    gradients = jnp.concatenate([key_all, value_all], axis=1).reshape(
        PAIRS, rows_per_block, 2 * key_value_width
    )
    summed = gradients[0]
    for offset in range(1, PAIRS):
        summed = summed + passed_along(
            gradients[offset].astype(jnp.bfloat16), "ctx", -offset
        ).astype(jnp.float32)
    key_grad = summed[:, :key_value_width].astype(jnp.bfloat16)
    value_grad = summed[:, key_value_width:].astype(jnp.bfloat16)
    return (attention, query_grad, key_grad, value_grad)


def solution(mesh):
    in_specs = (
        P(("ctx", "tp"), None),
        P(("ctx", "tp"), None),
        P(("ctx", "tp"), None),
        P(("ctx", "tp"), None),
        P(),
        P("ctx", None),
    )
    out_specs = (P("ctx", "tp"), P("ctx", "tp"), P("ctx", "tp"), P("ctx", "tp"))
    return jax.shard_map(local, mesh=mesh, in_specs=in_specs, out_specs=out_specs, check_vma=False)
```

profile of v0, /device:TPU:8, one launch (start us, length us, event | category | flops | bytes accessed | tf_op | source)
XLA Modules:
  0.0 219.0 jit_solution(923688659531777705)
XLA Ops:
  2.2 4.3 %all-to-all-start.1 = ((bf16[128,4,128]{2,0,1:T(8,128)(2,1)}), bf16[128,4,128]{2,0,1:T(8,128)(2,1)S(1)}, u32[]{:S(2)}, u32[]{:S(2)}) async-start(bf16[128,4,128]{2,0,1:T(8,128)(2,1)} %copy_bitcast_fusion.3), calls=%async_computation.1 | async-start | bytes 262144 | tf_op jit(solution)/shard_map/all_to_all | solution.py:77
  8.1 2.3 %copy.35 = bf16[128,4096]{0,1:T(8,128)(2,1)} copy(bf16[128,4096]{1,0:T(8,128)(2,1)} %param.11) | data formatting | bytes 2097152 | tf_op args[3]
  12.5 3.3 %all-to-all-start.2 = ((bf16[128,4,128]{2,0,1:T(8,128)(2,1)}), bf16[128,4,128]{2,0,1:T(8,128)(2,1)S(1)}, u32[]{:S(2)}, u32[]{:S(2)}) async-start(bf16[128,4,128]{2,0,1:T(8,128)(2,1)} %copy_bitcast_fusion.2), calls=%async_computation.2 | async-start | bytes 262144 | tf_op jit(solution)/shard_map/all_to_all | solution.py:78
  16.5 5.3 %all-to-all-done.2 = bf16[128,4,128]{2,0,1:T(8,128)(2,1)S(1)} async-done(((bf16[128,4,128]{2,0,1:T(8,128)(2,1)}), bf16[128,4,128]{2,0,1:T(8,128)(2,1)S(1)}, u32[]{:S(2)}, u32[]{:S(2)}) %all-to-all-start.2) | async-done | bytes 131104 | tf_op jit(solution)/shard_map/all_to_all | solution.py:78
  21.8 3.5 %all-to-all-start.3 = ((bf16[128,4,1024]{0,2,1:T(8,128)(2,1)}), bf16[128,4,1024]{0,2,1:T(8,128)(2,1)S(1)}, u32[]{:S(2)}, u32[]{:S(2)}) async-start(bf16[128,4,1024]{0,2,1:T(8,128)(2,1)} %bitcast.10), calls=%async_computation.3 | async-start | bytes 2097152 | tf_op jit(solution)/shard_map/all_to_all | solution.py:79
  33.8 3.8 %collective-permute-start.1 = (bf16[512,256]{1,0:T(8,128)(2,1)}, bf16[512,256]{1,0:T(8,128)(2,1)}, u32[]{:S(2)}, u32[]{:S(2)}) collective-permute-start(bf16[512,256]{1,0:T(8,128)(2,1)} %pad_maximum_fusion.1), channel_id=1, source_target_pairs={{0,8},{4,12},{8,16},{12,20},{16,24},{20,28},{24,32},{28,36},{32,40... | collective-permute-start | bytes 786440 | tf_op jit(solution)/shard_map/ppermute | solution.py:14
  37.6 5.2 %collective-permute-start.2 = (bf16[512,256]{1,0:T(8,128)(2,1)}, bf16[512,256]{1,0:T(8,128)(2,1)}, u32[]{:S(2)}, u32[]{:S(2)}) collective-permute-start(bf16[512,256]{1,0:T(8,128)(2,1)} %pad_maximum_fusion.1), channel_id=1, source_target_pairs={{0,12},{4,16},{8,20},{12,24},{16,28},{20,32},{24,36},{28,40},{32,4... | collective-permute-start | bytes 786440 | tf_op jit(solution)/shard_map/ppermute | solution.py:14
  42.8 4.7 %all-to-all-start = ((bf16[128,4,1024]{2,0,1:T(8,128)(2,1)}), bf16[128,4,1024]{2,0,1:T(8,128)(2,1)}, u32[]{:S(2)}, u32[]{:S(2)}) async-start(bf16[128,4,1024]{2,0,1:T(8,128)(2,1)} %bitcast.70), calls=%async_computation | async-start | bytes 2097152 | tf_op jit(solution)/shard_map/all_to_all | solution.py:76
  48.9 9.8 %collective-permute-done.2 = bf16[512,256]{1,0:T(8,128)(2,1)} collective-permute-done((bf16[512,256]{1,0:T(8,128)(2,1)}, bf16[512,256]{1,0:T(8,128)(2,1)}, u32[]{:S(2)}, u32[]{:S(2)}) %collective-permute-start.2) | collective-permute-done | bytes 262176 | tf_op jit(solution)/shard_map/ppermute | solution.py:14
  61.2 2.5 %copy.48 = bf16[64,8,8,128]{3,2,1,0:T(8,128)(2,1)} copy(bf16[64,8,8,128]{3,1,2,0:T(8,128)(2,1)} %bitcast.98) | data formatting | bytes 2097152
  68.0 124.7 %while.17 = (s32[]{:T(128)}, f32[2048,128]{1,0:T(8,128)}, f32[2048,128]{1,0:T(8,128)}, bf16[8,512,128]{1,2,0:T(8,128)(2,1)}, bf16[8,512,128]{2,1,0:T(8,128)(2,1)...) while((s32[]{:T(128)}, f32[2048,128]{1,0:T(8,128)}, ...), condition=%wide.region_4.5_spmd.clone, body=%wide.region_0.4_spmd.clone.sunk | while | flops 1624963584 | bytes 94520624 | solution.py:63
  75.2 2.8 %fusion.66 = f32[2048,128]{1,0:T(8,128)} fusion(bf16[512,2048]{1,0:T(8,128)(2,1)S(1)} %multiply_convert_fusion.2, f32[2048,128]{1,0:T(8,128)} %get-tuple-element.266, pred[]{:T(512)S(6)} %compare.3, bf16[8,512,128]{2,1,0:T(8,128)(2,1)} %get-tuple-element.282, s32[]{:T(128)} %get-tuple-element.265), kind=kOutput, calls=%fused_computation.7.clone.1 | convolution fusion | flops 269221888 | bytes 4325889 | tf_op jit(solution)/shard_map/while/body/eval_jaxpr/dot_general | solution.py:58
  80.1 2.8 %convolution_add_fusion.2 = f32[2048,128]{1,0:T(8,128)} fusion(f32[2048,128]{1,0:T(8,128)} %get-tuple-element.267, f32[512,2048]{1,0:T(8,128)S(1)} %copy-done.2, pred[]{:T(512)S(6)} %compare.3, bf16[8,512,128]{1,2,0:T(8,128)(2,1)} %copy-done.5, s32[]{:T(128)} %get-tuple-element.265), kind=kOutput, calls=%fused_computation.5.clone.1 | convolution fusion | flops 270008320 | bytes 6423041 | tf_op jit(solution)/shard_map/while/body/eval_jaxpr/dot_general | solution.py:59
  90.2 3.2 %fusion.66 = f32[2048,128]{1,0:T(8,128)} fusion(bf16[512,2048]{1,0:T(8,128)(2,1)S(1)} %multiply_convert_fusion.2, f32[2048,128]{1,0:T(8,128)} %get-tuple-element.266, pred[]{:T(512)S(6)} %compare.3, bf16[8,512,128]{2,1,0:T(8,128)(2,1)} %get-tuple-element.282, s32[]{:T(128)} %get-tuple-element.265), kind=kOutput, calls=%fused_computation.7.clone.1 | convolution fusion | flops 269221888 | bytes 4325889 | tf_op jit(solution)/shard_map/while/body/eval_jaxpr/dot_general | solution.py:58
  95.4 3.2 %convolution_add_fusion.2 = f32[2048,128]{1,0:T(8,128)} fusion(f32[2048,128]{1,0:T(8,128)} %get-tuple-element.267, f32[512,2048]{1,0:T(8,128)S(1)} %copy-done.2, pred[]{:T(512)S(6)} %compare.3, bf16[8,512,128]{1,2,0:T(8,128)(2,1)} %copy-done.5, s32[]{:T(128)} %get-tuple-element.265), kind=kOutput, calls=%fused_computation.5.clone.1 | convolution fusion | flops 270008320 | bytes 6423041 | tf_op jit(solution)/shard_map/while/body/eval_jaxpr/dot_general | solution.py:59
  98.6 2.1 fusion.63
  105.9 3.2 %fusion.66 = f32[2048,128]{1,0:T(8,128)} fusion(bf16[512,2048]{1,0:T(8,128)(2,1)S(1)} %multiply_convert_fusion.2, f32[2048,128]{1,0:T(8,128)} %get-tuple-element.266, pred[]{:T(512)S(6)} %compare.3, bf16[8,512,128]{2,1,0:T(8,128)(2,1)} %get-tuple-element.282, s32[]{:T(128)} %get-tuple-element.265), kind=kOutput, calls=%fused_computation.7.clone.1 | convolution fusion | flops 269221888 | bytes 4325889 | tf_op jit(solution)/shard_map/while/body/eval_jaxpr/dot_general | solution.py:58
  111.1 3.2 %convolution_add_fusion.2 = f32[2048,128]{1,0:T(8,128)} fusion(f32[2048,128]{1,0:T(8,128)} %get-tuple-element.267, f32[512,2048]{1,0:T(8,128)S(1)} %copy-done.2, pred[]{:T(512)S(6)} %compare.3, bf16[8,512,128]{1,2,0:T(8,128)(2,1)} %copy-done.5, s32[]{:T(128)} %get-tuple-element.265), kind=kOutput, calls=%fused_computation.5.clone.1 | convolution fusion | flops 270008320 | bytes 6423041 | tf_op jit(solution)/shard_map/while/body/eval_jaxpr/dot_general | solution.py:59
  121.6 3.2 %fusion.66 = f32[2048,128]{1,0:T(8,128)} fusion(bf16[512,2048]{1,0:T(8,128)(2,1)S(1)} %multiply_convert_fusion.2, f32[2048,128]{1,0:T(8,128)} %get-tuple-element.266, pred[]{:T(512)S(6)} %compare.3, bf16[8,512,128]{2,1,0:T(8,128)(2,1)} %get-tuple-element.282, s32[]{:T(128)} %get-tuple-element.265), kind=kOutput, calls=%fused_computation.7.clone.1 | convolution fusion | flops 269221888 | bytes 4325889 | tf_op jit(solution)/shard_map/while/body/eval_jaxpr/dot_general | solution.py:58
  126.8 3.2 %convolution_add_fusion.2 = f32[2048,128]{1,0:T(8,128)} fusion(f32[2048,128]{1,0:T(8,128)} %get-tuple-element.267, f32[512,2048]{1,0:T(8,128)S(1)} %copy-done.2, pred[]{:T(512)S(6)} %compare.3, bf16[8,512,128]{1,2,0:T(8,128)(2,1)} %copy-done.5, s32[]{:T(128)} %get-tuple-element.265), kind=kOutput, calls=%fused_computation.5.clone.1 | convolution fusion | flops 270008320 | bytes 6423041 | tf_op jit(solution)/shard_map/while/body/eval_jaxpr/dot_general | solution.py:59
  137.3 3.2 %fusion.66 = f32[2048,128]{1,0:T(8,128)} fusion(bf16[512,2048]{1,0:T(8,128)(2,1)S(1)} %multiply_convert_fusion.2, f32[2048,128]{1,0:T(8,128)} %get-tuple-element.266, pred[]{:T(512)S(6)} %compare.3, bf16[8,512,128]{2,1,0:T(8,128)(2,1)} %get-tuple-element.282, s32[]{:T(128)} %get-tuple-element.265), kind=kOutput, calls=%fused_computation.7.clone.1 | convolution fusion | flops 269221888 | bytes 4325889 | tf_op jit(solution)/shard_map/while/body/eval_jaxpr/dot_general | solution.py:58
  142.5 3.2 %convolution_add_fusion.2 = f32[2048,128]{1,0:T(8,128)} fusion(f32[2048,128]{1,0:T(8,128)} %get-tuple-element.267, f32[512,2048]{1,0:T(8,128)S(1)} %copy-done.2, pred[]{:T(512)S(6)} %compare.3, bf16[8,512,128]{1,2,0:T(8,128)(2,1)} %copy-done.5, s32[]{:T(128)} %get-tuple-element.265), kind=kOutput, calls=%fused_computation.5.clone.1 | convolution fusion | flops 270008320 | bytes 6423041 | tf_op jit(solution)/shard_map/while/body/eval_jaxpr/dot_general | solution.py:59
  153.0 3.2 %fusion.66 = f32[2048,128]{1,0:T(8,128)} fusion(bf16[512,2048]{1,0:T(8,128)(2,1)S(1)} %multiply_convert_fusion.2, f32[2048,128]{1,0:T(8,128)} %get-tuple-element.266, pred[]{:T(512)S(6)} %compare.3, bf16[8,512,128]{2,1,0:T(8,128)(2,1)} %get-tuple-element.282, s32[]{:T(128)} %get-tuple-element.265), kind=kOutput, calls=%fused_computation.7.clone.1 | convolution fusion | flops 269221888 | bytes 4325889 | tf_op jit(solution)/shard_map/while/body/eval_jaxpr/dot_general | solution.py:58
  158.2 3.2 %convolution_add_fusion.2 = f32[2048,128]{1,0:T(8,128)} fusion(f32[2048,128]{1,0:T(8,128)} %get-tuple-element.267, f32[512,2048]{1,0:T(8,128)S(1)} %copy-done.2, pred[]{:T(512)S(6)} %compare.3, bf16[8,512,128]{1,2,0:T(8,128)(2,1)} %copy-done.5, s32[]{:T(128)} %get-tuple-element.265), kind=kOutput, calls=%fused_computation.5.clone.1 | convolution fusion | flops 270008320 | bytes 6423041 | tf_op jit(solution)/shard_map/while/body/eval_jaxpr/dot_general | solution.py:59
  168.6 3.2 %fusion.66 = f32[2048,128]{1,0:T(8,128)} fusion(bf16[512,2048]{1,0:T(8,128)(2,1)S(1)} %multiply_convert_fusion.2, f32[2048,128]{1,0:T(8,128)} %get-tuple-element.266, pred[]{:T(512)S(6)} %compare.3, bf16[8,512,128]{2,1,0:T(8,128)(2,1)} %get-tuple-element.282, s32[]{:T(128)} %get-tuple-element.265), kind=kOutput, calls=%fused_computation.7.clone.1 | convolution fusion | flops 269221888 | bytes 4325889 | tf_op jit(solution)/shard_map/while/body/eval_jaxpr/dot_general | solution.py:58
  173.8 3.2 %convolution_add_fusion.2 = f32[2048,128]{1,0:T(8,128)} fusion(f32[2048,128]{1,0:T(8,128)} %get-tuple-element.267, f32[512,2048]{1,0:T(8,128)S(1)} %copy-done.2, pred[]{:T(512)S(6)} %compare.3, bf16[8,512,128]{1,2,0:T(8,128)(2,1)} %copy-done.5, s32[]{:T(128)} %get-tuple-element.265), kind=kOutput, calls=%fused_computation.5.clone.1 | convolution fusion | flops 270008320 | bytes 6423041 | tf_op jit(solution)/shard_map/while/body/eval_jaxpr/dot_general | solution.py:59
  184.3 3.2 %fusion.66 = f32[2048,128]{1,0:T(8,128)} fusion(bf16[512,2048]{1,0:T(8,128)(2,1)S(1)} %multiply_convert_fusion.2, f32[2048,128]{1,0:T(8,128)} %get-tuple-element.266, pred[]{:T(512)S(6)} %compare.3, bf16[8,512,128]{2,1,0:T(8,128)(2,1)} %get-tuple-element.282, s32[]{:T(128)} %get-tuple-element.265), kind=kOutput, calls=%fused_computation.7.clone.1 | convolution fusion | flops 269221888 | bytes 4325889 | tf_op jit(solution)/shard_map/while/body/eval_jaxpr/dot_general | solution.py:58
  189.5 3.2 %convolution_add_fusion.2 = f32[2048,128]{1,0:T(8,128)} fusion(f32[2048,128]{1,0:T(8,128)} %get-tuple-element.267, f32[512,2048]{1,0:T(8,128)S(1)} %copy-done.2, pred[]{:T(512)S(6)} %compare.3, bf16[8,512,128]{1,2,0:T(8,128)(2,1)} %copy-done.5, s32[]{:T(128)} %get-tuple-element.265), kind=kOutput, calls=%fused_computation.5.clone.1 | convolution fusion | flops 270008320 | bytes 6423041 | tf_op jit(solution)/shard_map/while/body/eval_jaxpr/dot_general | solution.py:59
  198.3 3.4 %collective-permute-start.4 = (bf16[512,256]{1,0:T(8,128)(2,1)}, bf16[512,256]{1,0:T(8,128)(2,1)}, u32[]{:S(2)}, u32[]{:S(2)}) collective-permute-start(bf16[512,256]{1,0:T(8,128)(2,1)} %get-tuple-element.162), channel_id=1, source_target_pairs={{8,0},{12,4},{16,8},{20,12},{24,16},{28,20},{32,24},{36,28},{40,32... | collective-permute-start | bytes 786440 | tf_op jit(solution)/shard_map/ppermute | solution.py:14
  201.7 4.4 %collective-permute-start.5 = (bf16[512,256]{1,0:T(8,128)(2,1)}, bf16[512,256]{1,0:T(8,128)(2,1)}, u32[]{:S(2)}, u32[]{:S(2)}) collective-permute-start(bf16[512,256]{1,0:T(8,128)(2,1)} %get-tuple-element.161), channel_id=1, source_target_pairs={{12,0},{16,4},{20,8},{24,12},{28,16},{32,20},{36,24},{40,28},{44,3... | collective-permute-start | bytes 786440 | tf_op jit(solution)/shard_map/ppermute | solution.py:14
  207.4 2.4 %copy_bitcast_fusion = bf16[512,1024]{1,0:T(8,128)(2,1)} fusion(bf16[8,512,128]{2,1,0:T(8,128)(2,1)} %get-tuple-element.60), kind=kLoop, calls=%fused_computation.30 | loop fusion | bytes 2097152 | tf_op jit(solution)/shard_map/reshape;stack | solution.py:103
  209.8 7.4 %collective-permute-done.5 = bf16[512,256]{1,0:T(8,128)(2,1)} collective-permute-done((bf16[512,256]{1,0:T(8,128)(2,1)}, bf16[512,256]{1,0:T(8,128)(2,1)}, u32[]{:S(2)}, u32[]{:S(2)}) %collective-permute-start.5) | collective-permute-done | bytes 262176 | tf_op jit(solution)/shard_map/ppermute | solution.py:14
  (195 shorter events, 100.7 us)
Async XLA Ops:
  0.6 15.2 %copy-start.9 = (s32[1,4]{1,0:T(1,128)S(1)}, s32[1,4]{1,0:T(1,128)}, u32[]{:S(2)}) copy-start(s32[1,4]{1,0:T(1,128)} %param.13) | copy-start | bytes 52
  2.2 10.3 %all-to-all-start.1 = ((bf16[128,4,128]{2,0,1:T(8,128)(2,1)}), bf16[128,4,128]{2,0,1:T(8,128)(2,1)S(1)}, u32[]{:S(2)}, u32[]{:S(2)}) async-start(bf16[128,4,128]{2,0,1:T(8,128)(2,1)} %copy_bitcast_fusion.3), calls=%async_computation.1 | async-start | bytes 262144 | tf_op jit(solution)/shard_map/all_to_all | solution.py:77
  8.1 19.8 %copy-start.7 = (bf16[128,4096]{1,0:T(8,128)(2,1)S(1)}, bf16[128,4096]{1,0:T(8,128)(2,1)}, u32[]{:S(2)}) copy-start(bf16[128,4096]{1,0:T(8,128)(2,1)} %param.8) | copy-start | bytes 3145732
  12.5 9.3 %all-to-all-start.2 = ((bf16[128,4,128]{2,0,1:T(8,128)(2,1)}), bf16[128,4,128]{2,0,1:T(8,128)(2,1)S(1)}, u32[]{:S(2)}, u32[]{:S(2)}) async-start(bf16[128,4,128]{2,0,1:T(8,128)(2,1)} %copy_bitcast_fusion.2), calls=%async_computation.2 | async-start | bytes 262144 | tf_op jit(solution)/shard_map/all_to_all | solution.py:78
  21.8 21.1 %all-to-all-start.3 = ((bf16[128,4,1024]{0,2,1:T(8,128)(2,1)}), bf16[128,4,1024]{0,2,1:T(8,128)(2,1)S(1)}, u32[]{:S(2)}, u32[]{:S(2)}) async-start(bf16[128,4,1024]{0,2,1:T(8,128)(2,1)} %bitcast.10), calls=%async_computation.3 | async-start | bytes 2097152 | tf_op jit(solution)/shard_map/all_to_all | solution.py:79
  31.9 15.8 %collective-permute-start = (bf16[512,256]{1,0:T(8,128)(2,1)}, bf16[512,256]{1,0:T(8,128)(2,1)}, u32[]{:S(2)}, u32[]{:S(2)}) collective-permute-start(bf16[512,256]{1,0:T(8,128)(2,1)} %pad_maximum_fusion.1), channel_id=1, source_target_pairs={{0,4},{4,8},{8,12},{12,16},{16,20},{20,24},{24,28},{28,32},{32,36}... | collective-permute-start | bytes 786440 | tf_op jit(solution)/shard_map/ppermute | solution.py:14
  33.8 15.1 %collective-permute-start.1 = (bf16[512,256]{1,0:T(8,128)(2,1)}, bf16[512,256]{1,0:T(8,128)(2,1)}, u32[]{:S(2)}, u32[]{:S(2)}) collective-permute-start(bf16[512,256]{1,0:T(8,128)(2,1)} %pad_maximum_fusion.1), channel_id=1, source_target_pairs={{0,8},{4,12},{8,16},{12,20},{16,24},{20,28},{24,32},{28,36},{32,40... | collective-permute-start | bytes 786440 | tf_op jit(solution)/shard_map/ppermute | solution.py:14
  37.6 21.0 %collective-permute-start.2 = (bf16[512,256]{1,0:T(8,128)(2,1)}, bf16[512,256]{1,0:T(8,128)(2,1)}, u32[]{:S(2)}, u32[]{:S(2)}) collective-permute-start(bf16[512,256]{1,0:T(8,128)(2,1)} %pad_maximum_fusion.1), channel_id=1, source_target_pairs={{0,12},{4,16},{8,20},{12,24},{16,28},{20,32},{24,36},{28,40},{32,4... | collective-permute-start | bytes 786440 | tf_op jit(solution)/shard_map/ppermute | solution.py:14
  42.8 22.5 %all-to-all-start = ((bf16[128,4,1024]{2,0,1:T(8,128)(2,1)}), bf16[128,4,1024]{2,0,1:T(8,128)(2,1)}, u32[]{:S(2)}, u32[]{:S(2)}) async-start(bf16[128,4,1024]{2,0,1:T(8,128)(2,1)} %bitcast.70), calls=%async_computation | async-start | bytes 2097152 | tf_op jit(solution)/shard_map/all_to_all | solution.py:76
  68.0 3.6 %copy-start.5 = (bf16[8,512,128]{1,2,0:T(8,128)(2,1)}, bf16[8,512,128]{1,2,0:T(8,128)(2,1)S(1)}, u32[]{:S(2)}) copy-start(bf16[8,512,128]{1,2,0:T(8,128)(2,1)S(1)} %get-tuple-element.285) | copy-start | bytes 3145732 | tf_op jit(solution)/shard_map/while
  75.2 4.8 %copy-start.2 = (f32[512,2048]{1,0:T(8,128)S(1)}, f32[512,2048]{1,0:T(8,128)}, u32[]{:S(2)}) copy-start(f32[512,2048]{1,0:T(8,128)} %copy-done.1) | copy-start | bytes 12582916 | tf_op jit(solution)/shard_map/while
  82.9 3.6 %copy-start.5 = (bf16[8,512,128]{1,2,0:T(8,128)(2,1)}, bf16[8,512,128]{1,2,0:T(8,128)(2,1)S(1)}, u32[]{:S(2)}) copy-start(bf16[8,512,128]{1,2,0:T(8,128)(2,1)S(1)} %get-tuple-element.285) | copy-start | bytes 3145732 | tf_op jit(solution)/shard_map/while
  90.2 5.2 %copy-start.2 = (f32[512,2048]{1,0:T(8,128)S(1)}, f32[512,2048]{1,0:T(8,128)}, u32[]{:S(2)}) copy-start(f32[512,2048]{1,0:T(8,128)} %copy-done.1) | copy-start | bytes 12582916 | tf_op jit(solution)/shard_map/while
  95.4 3.2 %copy-start.6 = (bf16[8,512,128]{1,2,0:T(8,128)(2,1)S(1)}, bf16[8,512,128]{1,2,0:T(8,128)(2,1)}, u32[]{:S(2)}) copy-start(bf16[8,512,128]{1,2,0:T(8,128)(2,1)} %copy-done.5) | copy-start | bytes 3145732 | tf_op jit(solution)/shard_map/while
  98.6 3.6 %copy-start.5 = (bf16[8,512,128]{1,2,0:T(8,128)(2,1)}, bf16[8,512,128]{1,2,0:T(8,128)(2,1)S(1)}, u32[]{:S(2)}) copy-start(bf16[8,512,128]{1,2,0:T(8,128)(2,1)S(1)} %get-tuple-element.285) | copy-start | bytes 3145732 | tf_op jit(solution)/shard_map/while
  105.9 5.2 %copy-start.2 = (f32[512,2048]{1,0:T(8,128)S(1)}, f32[512,2048]{1,0:T(8,128)}, u32[]{:S(2)}) copy-start(f32[512,2048]{1,0:T(8,128)} %copy-done.1) | copy-start | bytes 12582916 | tf_op jit(solution)/shard_map/while
  114.3 3.6 %copy-start.5 = (bf16[8,512,128]{1,2,0:T(8,128)(2,1)}, bf16[8,512,128]{1,2,0:T(8,128)(2,1)S(1)}, u32[]{:S(2)}) copy-start(bf16[8,512,128]{1,2,0:T(8,128)(2,1)S(1)} %get-tuple-element.285) | copy-start | bytes 3145732 | tf_op jit(solution)/shard_map/while
  121.6 5.2 %copy-start.2 = (f32[512,2048]{1,0:T(8,128)S(1)}, f32[512,2048]{1,0:T(8,128)}, u32[]{:S(2)}) copy-start(f32[512,2048]{1,0:T(8,128)} %copy-done.1) | copy-start | bytes 12582916 | tf_op jit(solution)/shard_map/while
  130.0 3.6 %copy-start.5 = (bf16[8,512,128]{1,2,0:T(8,128)(2,1)}, bf16[8,512,128]{1,2,0:T(8,128)(2,1)S(1)}, u32[]{:S(2)}) copy-start(bf16[8,512,128]{1,2,0:T(8,128)(2,1)S(1)} %get-tuple-element.285) | copy-start | bytes 3145732 | tf_op jit(solution)/shard_map/while
  137.3 5.2 %copy-start.2 = (f32[512,2048]{1,0:T(8,128)S(1)}, f32[512,2048]{1,0:T(8,128)}, u32[]{:S(2)}) copy-start(f32[512,2048]{1,0:T(8,128)} %copy-done.1) | copy-start | bytes 12582916 | tf_op jit(solution)/shard_map/while
  142.5 3.2 %copy-start.6 = (bf16[8,512,128]{1,2,0:T(8,128)(2,1)S(1)}, bf16[8,512,128]{1,2,0:T(8,128)(2,1)}, u32[]{:S(2)}) copy-start(bf16[8,512,128]{1,2,0:T(8,128)(2,1)} %copy-done.5) | copy-start | bytes 3145732 | tf_op jit(solution)/shard_map/while
  145.7 3.6 %copy-start.5 = (bf16[8,512,128]{1,2,0:T(8,128)(2,1)}, bf16[8,512,128]{1,2,0:T(8,128)(2,1)S(1)}, u32[]{:S(2)}) copy-start(bf16[8,512,128]{1,2,0:T(8,128)(2,1)S(1)} %get-tuple-element.285) | copy-start | bytes 3145732 | tf_op jit(solution)/shard_map/while
  152.9 5.2 %copy-start.2 = (f32[512,2048]{1,0:T(8,128)S(1)}, f32[512,2048]{1,0:T(8,128)}, u32[]{:S(2)}) copy-start(f32[512,2048]{1,0:T(8,128)} %copy-done.1) | copy-start | bytes 12582916 | tf_op jit(solution)/shard_map/while
  161.3 3.6 %copy-start.5 = (bf16[8,512,128]{1,2,0:T(8,128)(2,1)}, bf16[8,512,128]{1,2,0:T(8,128)(2,1)S(1)}, u32[]{:S(2)}) copy-start(bf16[8,512,128]{1,2,0:T(8,128)(2,1)S(1)} %get-tuple-element.285) | copy-start | bytes 3145732 | tf_op jit(solution)/shard_map/while
  168.6 5.2 %copy-start.2 = (f32[512,2048]{1,0:T(8,128)S(1)}, f32[512,2048]{1,0:T(8,128)}, u32[]{:S(2)}) copy-start(f32[512,2048]{1,0:T(8,128)} %copy-done.1) | copy-start | bytes 12582916 | tf_op jit(solution)/shard_map/while
  173.8 3.2 %copy-start.6 = (bf16[8,512,128]{1,2,0:T(8,128)(2,1)S(1)}, bf16[8,512,128]{1,2,0:T(8,128)(2,1)}, u32[]{:S(2)}) copy-start(bf16[8,512,128]{1,2,0:T(8,128)(2,1)} %copy-done.5) | copy-start | bytes 3145732 | tf_op jit(solution)/shard_map/while
  177.0 3.6 %copy-start.5 = (bf16[8,512,128]{1,2,0:T(8,128)(2,1)}, bf16[8,512,128]{1,2,0:T(8,128)(2,1)S(1)}, u32[]{:S(2)}) copy-start(bf16[8,512,128]{1,2,0:T(8,128)(2,1)S(1)} %get-tuple-element.285) | copy-start | bytes 3145732 | tf_op jit(solution)/shard_map/while
  184.3 5.2 %copy-start.2 = (f32[512,2048]{1,0:T(8,128)S(1)}, f32[512,2048]{1,0:T(8,128)}, u32[]{:S(2)}) copy-start(f32[512,2048]{1,0:T(8,128)} %copy-done.1) | copy-start | bytes 12582916 | tf_op jit(solution)/shard_map/while
  195.3 10.8 %copy-start.8 = (bf16[8,512,128]{1,2,0:T(8,128)(2,1)S(1)}, bf16[8,512,128]{1,2,0:T(8,128)(2,1)}, u32[]{:S(2)}) copy-start(bf16[8,512,128]{1,2,0:T(8,128)(2,1)} %get-tuple-element.59) | copy-start | bytes 3145732
  196.3 13.4 %collective-permute-start.3 = (bf16[512,256]{1,0:T(8,128)(2,1)}, bf16[512,256]{1,0:T(8,128)(2,1)S(1)}, u32[]{:S(2)}, u32[]{:S(2)}) collective-permute-start(bf16[512,256]{1,0:T(8,128)(2,1)} %get-tuple-element.160), channel_id=1, source_target_pairs={{4,0},{8,4},{12,8},{16,12},{20,16},{24,20},{28,24},{32,28},{36,32}... | collective-permute-start | bytes 786440 | tf_op jit(solution)/shard_map/ppermute | solution.py:14
  198.3 11.5 %collective-permute-start.4 = (bf16[512,256]{1,0:T(8,128)(2,1)}, bf16[512,256]{1,0:T(8,128)(2,1)}, u32[]{:S(2)}, u32[]{:S(2)}) collective-permute-start(bf16[512,256]{1,0:T(8,128)(2,1)} %get-tuple-element.162), channel_id=1, source_target_pairs={{8,0},{12,4},{16,8},{20,12},{24,16},{28,20},{32,24},{36,28},{40,32... | collective-permute-start | bytes 786440 | tf_op jit(solution)/shard_map/ppermute | solution.py:14
  201.7 15.5 %collective-permute-start.5 = (bf16[512,256]{1,0:T(8,128)(2,1)}, bf16[512,256]{1,0:T(8,128)(2,1)}, u32[]{:S(2)}, u32[]{:S(2)}) collective-permute-start(bf16[512,256]{1,0:T(8,128)(2,1)} %get-tuple-element.161), channel_id=1, source_target_pairs={{12,0},{16,4},{20,8},{24,12},{28,16},{32,20},{36,24},{40,28},{44,3... | collective-permute-start | bytes 786440 | tf_op jit(solution)/shard_map/ppermute | solution.py:14
  (30 other events, 73.6 us)
where the time goes:
time: 222 us; the launch traced here: 219 us
  matrix products  97.7 us (44%)
  local copies, waits for them, and re-layouts  38.3 us (17%)
  starting transfers between devices  36.5 us (16%)
  waiting for transfers between devices  25.6 us (12%)
  other arithmetic  17 us (8%)
  between operations  3.45 us (2%)
    dot_general x8, matrix products, one_head(): jnp.dot(probs_low.T, grad_one, preferred_element_type=jnp.float32)  25.1 us
    dot_general x8, matrix products, one_head(): jnp.dot(score_grad.T, query_one, preferred_element_type=jnp.float32)  24.9 us
    ppermute x6, starting transfers between devices, passed_along(): lax.ppermute(value, axis, [(source, source + steps) for source in range(i...  20.6 us
    ppermute x6, waiting for transfers between devices, passed_along(): lax.ppermute(value, axis, [(source, source + steps) for source in range(i...  18.3 us
    dot_general x8, matrix products, one_head(): jnp.dot(query_one, key_grp.T, preferred_element_type=jnp.float32) * scaling  16.4 us
    dot_general x8, matrix products, one_head(): jnp.dot(grad_one, value_grp.T, preferred_element_type=jnp.float32)  13.6 us
    unnamed x14, local copies, waits for them, and re-layouts  11.3 us
    dot_general x8, matrix products, one_head(): jnp.dot(score_grad, key_grp, preferred_element_type=jnp.float32) * scaling  10.9 us
  transfers between devices with their start and end apart: 10, of which 5 were waited for; matrix products, arithmetic and copies ran while one was open for 9% of the time, Pallas kernels for 0%

commit v1 on v0

v1 whole, which is shorter than its diff:
```python
import functools
import math

import jax
import jax.numpy as jnp
from jax import lax
from jax.experimental import pallas as pl
from jax.experimental.pallas import tpu as pltpu
from jax.sharding import PartitionSpec as P

HEAD_SIZE = 128
HEADS_PER_GROUP = 8
PAIRS = 4
BLOCK = 512
TQ = 128
TILES = BLOCK // TQ
LANES = HEADS_PER_GROUP * TQ
TK = 256
STEPS = BLOCK // TK
MOST_STEPS = TILES * PAIRS * STEPS
OFFSETS = (3, 2, 1, 0)
SUMS = HEAD_SIZE + 8
SCALING = HEAD_SIZE ** (-0.5)
LOG2_SCALING = SCALING * math.log2(math.e)
MASKED = -2e30
LOWEST = -1e30
F32 = jnp.float32
BF16 = jnp.bfloat16


def dot_nt(a, b):
    return lax.dot_general(a, b, (((1,), (1,)), ((), ())), preferred_element_type=F32)


def dot_nn(a, b):
    return lax.dot_general(a, b, (((1,), (0,)), ((), ())), preferred_element_type=F32)


def tile_bias(lo_row, tile, key_start):
    keys = lax.broadcasted_iota(jnp.int32, (TK, TQ), 0) + key_start
    last = lax.broadcasted_iota(jnp.int32, (TK, TQ), 1) + ((PAIRS - 1) * BLOCK + tile * TQ)
    return jnp.where((keys >= lo_row) & (keys <= last), 0.0, MASKED).astype(F32)


def list_steps(scalars, meta):
    count = jnp.int32(0)
    for slot, offset in enumerate(OFFSETS):
        base = (PAIRS - 1 - offset) * BLOCK
        for tile in range(TILES):
            last = (tile * TQ) // TK + 1 if offset == 0 else STEPS
            first = jnp.minimum(jnp.maximum(scalars[tile] - base, 0) // TK, last)
            first = jnp.where(scalars[TILES + offset] == 1, first, last)

            def write(i, n, slot=slot, tile=tile, base=base):
                meta[0, n] = tile
                meta[1, n] = slot * STEPS + i
                meta[2, n] = base + i * TK
                return n + 1

            count = lax.fori_loop(first, last, write, count)
    for extra in range(2):
        meta[0, count + extra] = 0
        meta[1, count + extra] = 0
        meta[2, count + extra] = PAIRS * BLOCK
    return count


def run_steps(count, stage1, stage2, buf_a, buf_b):
    stage1(0, buf_a)

    def body(j, carry):
        stage1(2 * j + 1, buf_b)
        stage2(2 * j, buf_a)
        stage1(2 * j + 2, buf_a)
        stage2(2 * j + 1, buf_b)
        return carry

    lax.fori_loop(0, (count + 1) // 2, body, 0)


def rows_of(k):
    return pl.ds(pl.multiple_of(k * TK, TK), TK)


def pack_kernel(*refs):
    refs, out_ref = refs[:-1], refs[-1]
    groups = out_ref.shape[0]
    slot = 0
    for ref in refs:
        per_group = ref.shape[1] // HEAD_SIZE // groups
        for group in range(groups):
            for h in range(per_group):
                head = group * per_group + h
                out_ref[group, slot + h] = ref[:, head * HEAD_SIZE : (head + 1) * HEAD_SIZE]
        slot += per_group


def attend_kernel(heads, first_head, first_call, last_call, scalars, x_ref, *refs):
    kvs, lo_ref, refs = refs[0:PAIRS], refs[PAIRS], refs[PAIRS + 1 :]
    if not first_call:
        dk_in, dv_in, refs = refs[0], refs[1], refs[4:]
    att_ref, dq_ref, refs = refs[0], refs[1], refs[2:]
    if last_call:
        outs, refs = refs[0:PAIRS], refs[PAIRS:]
    else:
        dk_out, dv_out, refs = refs[0], refs[1], refs[2:]
    m_s, acc_s, dqt_s, dk_s, dv_s, delta_s, k_s, kt_s, v_s, vt_s = refs[:10]
    buf_a, buf_b, stash_s, top_s, att_s, meta, sem = refs[10:]
    lanes_all = heads * TQ
    if not last_call:
        dk_s, dv_s = dk_out, dv_out

    def queries(tile):
        return x_ref[tile, 0:heads].reshape(lanes_all, HEAD_SIZE)

    def cotangents(tile):
        return x_ref[tile, heads : 2 * heads].reshape(lanes_all, HEAD_SIZE)

    def columns(h):
        return slice(h * TQ, (h + 1) * TQ)

    def put(tile, ref, kind):
        return pltpu.make_async_copy(
            att_s.at[tile],
            ref.at[pl.ds(tile * TQ, TQ), pl.ds(first_head * TQ, lanes_all)],
            sem.at[kind, tile],
        )

    for slot, kv in enumerate(reversed(kvs)):
        for part in range(TILES):
            place = slice(slot * BLOCK + part * TQ, slot * BLOCK + (part + 1) * TQ)
            key, value = kv[part, 0], kv[part, 1]
            k_s[place, :] = key
            kt_s[:, place] = key.T
            v_s[place, :] = value
            vt_s[0:HEAD_SIZE, place] = value.T
    vt_s[HEAD_SIZE:SUMS, :] = jnp.ones((SUMS - HEAD_SIZE, PAIRS * BLOCK), BF16)
    m_s[...] = jnp.full_like(m_s, LOWEST)
    acc_s[...] = jnp.zeros_like(acc_s)
    count = list_steps(scalars, meta)

    def scores(n, buf):
        buf[...] = dot_nt(k_s[rows_of(meta[1, n]), :], queries(meta[0, n]))

    def weigh(n, buf):
        tile = meta[0, n]
        bias = tile_bias(lo_ref[tile], tile, meta[2, n])
        val_t = vt_s[:, rows_of(meta[1, n])]
        m_old = m_s[tile]
        weights, tops = [], []
        for h in range(heads):
            s = buf[:, columns(h)] * LOG2_SCALING + bias
            top = jnp.maximum(m_old[:, columns(h)], jnp.max(s, axis=0, keepdims=True))
            weights.append(jnp.exp2(s - top).astype(BF16))
            tops.append(top)
        p = jnp.concatenate(weights, axis=1)
        m_new = jnp.concatenate(tops, axis=1)
        stash_s[n] = p
        top_s[n] = m_new
        m_s[tile] = m_new
        acc_s[tile] = acc_s[tile] * jnp.exp2(m_old - m_new) + dot_nn(val_t, p)

    run_steps(count, scores, weigh, buf_a, buf_b)
    ones = jnp.ones((8, HEAD_SIZE), BF16)
    for tile in range(TILES):
        total = acc_s[tile, HEAD_SIZE : HEAD_SIZE + 1, :]
        m_s[tile] = m_s[tile] + jnp.log2(total)
        inverse = 1.0 / total
        for h in range(heads):
            out = (acc_s[tile, 0:HEAD_SIZE, columns(h)] * inverse[:, columns(h)]).astype(BF16).T
            att_s[tile, :, columns(h)] = out
            product = out.astype(F32) * x_ref[tile, heads + h].astype(F32)
            high = product.astype(BF16)
            low = (product - high.astype(F32)).astype(BF16)
            delta_s[tile, :, columns(h)] = (dot_nt(ones, high) + dot_nt(ones, low))[0:1]
        put(tile, att_ref, 0).start()
    if first_call:
        dk_s[...] = jnp.zeros_like(dk_s)
        dv_s[...] = jnp.zeros_like(dv_s)
    else:
        dk_s[...] = dk_in[...]
        dv_s[...] = dv_in[...]
    dqt_s[...] = jnp.zeros_like(dqt_s)

    def prob_grads(n, buf):
        buf[...] = dot_nt(v_s[rows_of(meta[1, n]), :], cotangents(meta[0, n]))

    def gradients(n, buf):
        tile, rows = meta[0, n], rows_of(meta[1, n])
        factor = jnp.exp2(top_s[n] - m_s[tile])
        delta = delta_s[tile]
        weights, grads = [], []
        for h in range(heads):
            p = stash_s[n, :, columns(h)].astype(F32) * factor[:, columns(h)]
            weights.append(p.astype(BF16))
            grads.append((p * (buf[:, columns(h)] - delta[:, columns(h)])).astype(BF16))
        p = jnp.concatenate(weights, axis=1)
        g = jnp.concatenate(grads, axis=1)
        dv_s[rows, :] += dot_nn(p, cotangents(tile))
        dk_s[rows, :] += dot_nn(g, queries(tile))
        dqt_s[tile] += dot_nn(kt_s[:, rows], g)

    run_steps(count, prob_grads, gradients, buf_a, buf_b)
    for tile in range(TILES):
        put(tile, att_ref, 0).wait()
        for h in range(heads):
            att_s[tile, :, columns(h)] = (dqt_s[tile, :, columns(h)] * SCALING).astype(BF16).T
        put(tile, dq_ref, 1).start()
    if last_call:
        for slot in range(PAIRS):
            kind = outs[slot].dtype
            for part in range(TILES):
                place = slice(slot * BLOCK + part * TQ, slot * BLOCK + (part + 1) * TQ)
                outs[slot][part, 0] = (dk_s[place, :] * SCALING).astype(kind)
                outs[slot][part, 1] = dv_s[place, :].astype(kind)
    for tile in range(TILES):
        put(tile, dq_ref, 1).wait()


def vmem():
    return pl.BlockSpec(memory_space=pltpu.VMEM)


def smem():
    return pl.BlockSpec(memory_space=pltpu.SMEM)


def pack(*arrays, steps=1, limit=40):
    heads = sum(array.shape[1] // HEAD_SIZE // TILES for array in arrays)
    tokens = arrays[0].shape[0]
    return pl.pallas_call(
        pack_kernel,
        grid=(steps,),
        in_specs=[
            pl.BlockSpec((tokens, array.shape[1] // steps), lambda g: (0, g)) for array in arrays
        ],
        out_specs=pl.BlockSpec(
            (TILES // steps, heads, tokens, HEAD_SIZE), lambda g: (g, 0, 0, 0)
        ),
        out_shape=jax.ShapeDtypeStruct((TILES, heads, tokens, HEAD_SIZE), BF16),
        compiler_params=pltpu.CompilerParams(vmem_limit_bytes=limit << 20),
        name="pack_%d" % len(arrays),
    )(*arrays)


def attend(scalars, x, kvs, lo, first_head, carried):
    rows = PAIRS * BLOCK
    heads = x.shape[1] // 2
    lanes = heads * TQ
    first_call, last_call = not carried, first_head + heads == HEADS_PER_GROUP
    hbm = pl.BlockSpec(memory_space=pltpu.HBM)
    result = jax.ShapeDtypeStruct((BLOCK, LANES), BF16)
    sums = [jax.ShapeDtypeStruct((rows, HEAD_SIZE), F32)] * 2
    grad_shape = (TILES, 2, TQ, HEAD_SIZE)
    parts = [jax.ShapeDtypeStruct(grad_shape, F32 if o == 0 else BF16) for o in OFFSETS]
    more = parts if last_call else sums
    return pl.pallas_call(
        functools.partial(attend_kernel, heads, first_head, first_call, last_call),
        in_specs=[smem()] + [vmem()] * (PAIRS + 2) + [vmem(), vmem(), hbm, hbm][: len(carried)],
        out_specs=[hbm, hbm] + [vmem()] * len(more),
        out_shape=[result, result] + more,
        input_output_aliases={} if first_call else {PAIRS + 5: 0, PAIRS + 6: 1},
        scratch_shapes=[
            pltpu.VMEM((TILES, 1, lanes), F32),
            pltpu.VMEM((TILES, SUMS, lanes), F32),
            pltpu.VMEM((TILES, HEAD_SIZE, lanes), F32),
            pltpu.VMEM((rows if last_call else 8, HEAD_SIZE), F32),
            pltpu.VMEM((rows if last_call else 8, HEAD_SIZE), F32),
            pltpu.VMEM((TILES, 1, lanes), F32),
            pltpu.VMEM((rows, HEAD_SIZE), BF16),
            pltpu.VMEM((HEAD_SIZE, rows), BF16),
            pltpu.VMEM((rows, HEAD_SIZE), BF16),
            pltpu.VMEM((SUMS, rows), BF16),
            pltpu.VMEM((TK, lanes), F32),
            pltpu.VMEM((TK, lanes), F32),
            pltpu.VMEM((MOST_STEPS, TK, lanes), BF16),
            pltpu.VMEM((MOST_STEPS, 1, lanes), F32),
            pltpu.VMEM((TILES, TQ, lanes), BF16),
            pltpu.SMEM((3, MOST_STEPS), jnp.int32),
            pltpu.SemaphoreType.DMA((2, TILES)),
        ],
        compiler_params=pltpu.CompilerParams(vmem_limit_bytes=(12 + 3 * heads) << 20),
        cost_estimate=pl.CostEstimate(
            flops=2 * 6 * heads * 512 * 1280 * 128 * 2, bytes_accessed=8 << 20, transcendentals=0
        ),
        name="attend_%d" % first_head,
    )(scalars, x, *kvs, lo, *carried)


def passed_along(value, axis, steps):
    count = lax.axis_size(axis)
    initial, last = (max(0, -steps), min(count, count - steps))
    return lax.ppermute(value, axis, [(source, source + steps) for source in range(initial, last)])


def exchange(value):
    return lax.all_to_all(value, "tp", split_axis=0, concat_axis=0, tiled=True)


def window_start(doc_ids, blk):
    begin = jnp.maximum(blk - (PAIRS - 1), 0) * BLOCK
    window = lax.dynamic_slice_in_dim(doc_ids, begin, PAIRS * BLOCK)
    own = lax.dynamic_slice_in_dim(doc_ids, blk * BLOCK, BLOCK)
    before = jnp.sum((window[:, None] < own[None, :]).astype(jnp.int32), axis=0)
    return before + begin - (blk - (PAIRS - 1)) * BLOCK


def bounds(lo, live):
    return lo.reshape(TILES, 1, TQ), jnp.concatenate([lo[::TQ], live])


def local(queries, key_states, value_projection, output_gradient, doc_ids, pair_live):
    blk = lax.axis_index("ctx")
    kv0 = exchange(pack(key_states, value_projection, limit=60))
    x = exchange(pack(queries, output_gradient, steps=4, limit=60))
    lo, scalars = bounds(window_start(doc_ids, blk), pair_live[0])
    kv2 = passed_along(kv0, "ctx", 2)
    kv1 = passed_along(kv0, "ctx", 1)
    kv3 = passed_along(kv2, "ctx", 1)
    kvs = [kv0, kv1, kv2, kv3]
    attention, dq, part3, part2, part1, part0 = attend(scalars, x, kvs, lo, 0, ())
    got3 = passed_along(part3, "ctx", -1)
    got1 = passed_along(part1, "ctx", -1)
    part2 = (part2.astype(F32) + got3.astype(F32)).astype(BF16)
    got2 = passed_along(part2, "ctx", -2)
    total = part0 + got1.astype(F32) + got2.astype(F32)
    key_grad = total[:, 0].reshape(BLOCK, HEAD_SIZE).astype(BF16)
    value_grad = total[:, 1].reshape(BLOCK, HEAD_SIZE).astype(BF16)
    return (attention, dq, key_grad, value_grad)


def solution(mesh):
    in_specs = (
        P(("ctx", "tp"), None),
        P(("ctx", "tp"), None),
        P(("ctx", "tp"), None),
        P(("ctx", "tp"), None),
        P(),
        P("ctx", None),
    )
    out_specs = (P("ctx", "tp"), P("ctx", "tp"), P("ctx", "tp"), P("ctx", "tp"))
    return jax.shard_map(local, mesh=mesh, in_specs=in_specs, out_specs=out_specs, check_vma=False)
```

time: 222 us -> 91.5 us (0.41); the launches traced: 219 us -> 91.2 us
  matrix products: 97.7 us -> 0 us
  local copies, waits for them, and re-layouts: 38.3 us -> 2.36 us
  Pallas kernels: 0 us -> 16.6 us
  other arithmetic: 17 us -> 0.81 us
  starting transfers between devices: 36.5 us -> 48.8 us
  waiting for transfers between devices: 25.6 us -> 21.8 us
  between operations: 3.45 us -> 0.75 us
    dot_general x48 -> x0, matrix products: 97.7 us -> none  [the longest x8 25.1 us: one_head(): jnp.dot(probs_low.T, grad_one, preferred_element_type=jnp.float32)]
    ppermute x6, starting transfers between devices: 20.6 us -> 40.9 us  [passed_along(): lax.ppermute(value, axis, [(source, source + steps) for source in range(i...]
    pallas_call x0 -> x3, Pallas kernels: none -> 16.6 us  [the longest x1 11 us: attend(): pl.pallas_call(functools.partial(attend_kernel, heads, first_head, first_...]
    unnamed x14 -> x2, local copies, waits for them, and re-layouts: 11.3 us -> 0.01 us
    while x96 -> x0, local copies, waits for them, and re-layouts: 8.75 us -> none
    all_to_all x4 -> x2, starting transfers between devices: 15.9 us -> 7.9 us  [exchange(): return lax.all_to_all(value, 'tp', split_axis=0, concat_axis=0, tiled=True)]
    div x8 -> x0, other arithmetic: 6.76 us -> none  [one_head(): attn_probs = exponent / jnp.sum(exponent, axis=1, keepdims=True)]
    dynamic_update_slice x8 -> x0, local copies, waits for them, and re-layouts: 5.37 us -> none  [attend(): lax.scan(one_head, (empty, empty), (query_seq, grad_seq))]
  transfers between devices with their start and end apart: 10 -> 8, of which waited for: 5 -> 6; matrix products, arithmetic and copies ran while one was open for 9% -> 3% of each run, Pallas kernels for 0% -> 4%
where the time goes in v1:
time: 91.5 us; the launch traced here: 91.2 us
  starting transfers between devices  48.8 us (53%)
  waiting for transfers between devices  21.8 us (24%)
  Pallas kernels  16.6 us (18%)
  local copies, waits for them, and re-layouts  2.36 us (3%)
    ppermute x6, starting transfers between devices, passed_along(): lax.ppermute(value, axis, [(source, source + steps) for source in range(i...  40.9 us
    ppermute x6, waiting for transfers between devices, passed_along(): lax.ppermute(value, axis, [(source, source + steps) for source in range(i...  16.2 us
    pallas_call x1, Pallas kernels, attend(): pl.pallas_call(functools.partial(attend_kernel, heads, first_head, first_...  11 us
    all_to_all x2, starting transfers between devices, exchange(): return lax.all_to_all(value, 'tp', split_axis=0, concat_axis=0, tiled=True)  7.9 us
    all_to_all x2, waiting for transfers between devices, exchange(): return lax.all_to_all(value, 'tp', split_axis=0, concat_axis=0, tiled=True)  5.64 us
    pallas_call x2, Pallas kernels, pack(): pl.pallas_call(pack_kernel, grid=(steps,), in_specs=[pl.BlockSpec((tokens...  5.59 us
  transfers between devices with their start and end apart: 8, of which 6 were waited for; matrix products, arithmetic and copies ran while one was open for 3% of the time, Pallas kernels for 4%

profile of v1, /device:TPU:8, one launch (start us, length us, event | category | flops | bytes accessed | tf_op | source)
XLA Modules:
  0.0 91.2 jit_solution(12385869060236390556)
XLA Ops:
  0.6 1.7 %pack_2.3 = bf16[4,2,128,128]{3,2,1,0:T(8,128)(2,1)} custom-call(bf16[128,512]{1,0:T(8,128)(2,1)} %refs_0_.3, bf16[128,512]{1,0:T(8,128)(2,1)} %refs_1_.3), custom_call_target="tpu_custom_call" | custom-call | tf_op jit(solution)/shard_map/pack_2/pallas_call | solution.py:231
  2.3 4.3 %all-to-all-start.1 = ((bf16[4,2,128,128]{3,2,1,0:T(8,128)(2,1)}), bf16[4,2,128,128]{3,2,1,0:T(8,128)(2,1)S(1)}, u32[]{:S(2)}, u32[]{:S(2)}) async-start(bf16[4,2,128,128]{3,2,1,0:T(8,128)(2,1)} %pack_2.3), calls=%async_computation.1 | async-start | bytes 524288 | tf_op jit(solution)/shard_map/all_to_all | solution.py:297
  6.6 3.9 %pack_2.2 = bf16[4,16,128,128]{3,2,1,0:T(8,128)(2,1)} custom-call(bf16[128,4096]{1,0:T(8,128)(2,1)} %refs_0_.2, bf16[128,4096]{1,0:T(8,128)(2,1)} %refs_1_.2), custom_call_target="tpu_custom_call" | custom-call | tf_op jit(solution)/shard_map/pack_2/pallas_call | solution.py:231
  10.5 0.0 copy-start
  10.5 2.8 %all-to-all-done.1.refs_0_ = bf16[4,2,128,128]{3,2,1,0:T(8,128)(2,1)S(1)} async-done(((bf16[4,2,128,128]{3,2,1,0:T(8,128)(2,1)}), bf16[4,2,128,128]{3,2,1,0:T(8,128)(2,1)S(1)}, u32[]{:S(2)}, u32[]{:S(2)}) %all-to-all-start.1) | async-done | bytes 262176 | tf_op jit(solution)/shard_map/all_to_all | solution.py:297
  13.3 3.6 %all-to-all-start = ((bf16[4,16,128,128]{3,2,1,0:T(8,128)(2,1)}), bf16[4,16,128,128]{3,2,1,0:T(8,128)(2,1)S(1)}, u32[]{:S(2)}, u32[]{:S(2)}) async-start(bf16[4,16,128,128]{3,2,1,0:T(8,128)(2,1)} %pack_2.2), calls=%async_computation | async-start | bytes 4194304 | tf_op jit(solution)/shard_map/all_to_all | solution.py:297
  16.9 3.8 %collective-permute-start.1 = (bf16[4,2,128,128]{3,2,1,0:T(8,128)(2,1)S(1)}, bf16[4,2,128,128]{3,2,1,0:T(8,128)(2,1)S(1)}, u32[]{:S(2)}, u32[]{:S(2)}) collective-permute-start(bf16[4,2,128,128]{3,2,1,0:T(8,128)(2,1)S(1)} %all-to-all-done.1.refs_0_), channel_id=1, source_target_pairs={{0,8},{4,12},{8,16},{12,20},{16,24},{20,28},{24,32},{28,36},{32,40... | collective-permute-start | bytes 786440 | tf_op jit(solution)/shard_map/ppermute | solution.py:293
  20.8 0.8 dynamic_slice.7
  21.5 0.8 dynamic_slice.6
  22.3 0.6 convert_reduce_fusion
  22.9 1.9 %collective-permute-start = (bf16[4,2,128,128]{3,2,1,0:T(8,128)(2,1)S(1)}, bf16[4,2,128,128]{3,2,1,0:T(8,128)(2,1)S(1)}, u32[]{:S(2)}, u32[]{:S(2)}) collective-permute-start(bf16[4,2,128,128]{3,2,1,0:T(8,128)(2,1)S(1)} %all-to-all-done.1.refs_0_), channel_id=1, source_target_pairs={{0,4},{4,8},{8,12},{12,16},{16,20},{20,24},{24,28},{28,32},{32,36}... | collective-permute-start | bytes 786440 | tf_op jit(solution)/shard_map/ppermute | solution.py:293
  24.8 4.7 %collective-permute-done.1.refs_2_ = bf16[4,2,128,128]{3,2,1,0:T(8,128)(2,1)S(1)} collective-permute-done((bf16[4,2,128,128]{3,2,1,0:T(8,128)(2,1)S(1)}, bf16[4,2,128,128]{3,2,1,0:T(8,128)(2,1)S(1)}, u32[]{:S(2)}, u32[]{:S(2)}) %collective-permute-start.1) | collective-permute-done | bytes 262176 | tf_op jit(solution)/shard_map/ppermute | solution.py:293
  29.5 1.9 %collective-permute-start.2 = (bf16[4,2,128,128]{3,2,1,0:T(8,128)(2,1)S(1)}, bf16[4,2,128,128]{3,2,1,0:T(8,128)(2,1)S(1)}, u32[]{:S(2)}, u32[]{:S(2)}) collective-permute-start(bf16[4,2,128,128]{3,2,1,0:T(8,128)(2,1)S(1)} %collective-permute-done.1.refs_2_), channel_id=1, source_target_pairs={{0,4},{4,8},{8,12},{12,16},{16,20},{20,24},{24,28},{28,32},{32,36}... | collective-permute-start | bytes 786440 | tf_op jit(solution)/shard_map/ppermute | solution.py:293
  31.4 0.1 slice.11
  31.5 0.0 copy-done
  31.5 0.1 pad_add_fusion.scalars
  31.6 1.1 %collective-permute-done.refs_1_ = bf16[4,2,128,128]{3,2,1,0:T(8,128)(2,1)S(1)} collective-permute-done((bf16[4,2,128,128]{3,2,1,0:T(8,128)(2,1)S(1)}, bf16[4,2,128,128]{3,2,1,0:T(8,128)(2,1)S(1)}, u32[]{:S(2)}, u32[]{:S(2)}) %collective-permute-start) | collective-permute-done | bytes 262176 | tf_op jit(solution)/shard_map/ppermute | solution.py:293
  32.7 6.6 %collective-permute-done.2.refs_3_ = bf16[4,2,128,128]{3,2,1,0:T(8,128)(2,1)S(1)} collective-permute-done((bf16[4,2,128,128]{3,2,1,0:T(8,128)(2,1)S(1)}, bf16[4,2,128,128]{3,2,1,0:T(8,128)(2,1)S(1)}, u32[]{:S(2)}, u32[]{:S(2)}) %collective-permute-start.2) | collective-permute-done | bytes 262176 | tf_op jit(solution)/shard_map/ppermute | solution.py:293
  39.3 2.8 %all-to-all-done.x_ref = bf16[4,16,128,128]{3,2,1,0:T(8,128)(2,1)S(1)} async-done(((bf16[4,16,128,128]{3,2,1,0:T(8,128)(2,1)}), bf16[4,16,128,128]{3,2,1,0:T(8,128)(2,1)S(1)}, u32[]{:S(2)}, u32[]{:S(2)}) %all-to-all-start) | async-done | bytes 2097184 | tf_op jit(solution)/shard_map/all_to_all | solution.py:297
  42.1 11.0 %attend_0.1 = (bf16[512,1024]{1,0:T(8,128)(2,1)}, bf16[512,1024]{1,0:T(8,128)(2,1)}, bf16[4,2,128,128]{3,2,1,0:T(8,128)(2,1)S(1)}, bf16[4,2,128,128]{3,2,1,0:T(8...) custom-call(s32[8]{0:T(128)S(1)} %pad_add_fusion.scalars, ...), custom_call_target="tpu_custom_call" | custom-call | flops 16106127360 | bytes 8388608 | tf_op jit(solution)/shard_map/attend_0/pallas_call | solution.py:257
  53.1 4.8 %collective-permute-start.4 = (bf16[4,2,128,128]{3,2,1,0:T(8,128)(2,1)S(1)}, bf16[4,2,128,128]{3,2,1,0:T(8,128)(2,1)S(1)}, u32[]{:S(2)}, u32[]{:S(2)}) collective-permute-start(bf16[4,2,128,128]{3,2,1,0:T(8,128)(2,1)S(1)} %get-tuple-element.15), channel_id=1, source_target_pairs={{4,0},{8,4},{12,8},{16,12},{20,16},{24,20},{28,24},{32,28},{36,32}... | collective-permute-start | bytes 786440 | tf_op jit(solution)/shard_map/ppermute | solution.py:293
  57.9 7.0 %collective-permute-start.3 = (bf16[4,2,128,128]{3,2,1,0:T(8,128)(2,1)S(1)}, bf16[4,2,128,128]{3,2,1,0:T(8,128)(2,1)S(1)}, u32[]{:S(2)}, u32[]{:S(2)}) collective-permute-start(bf16[4,2,128,128]{3,2,1,0:T(8,128)(2,1)S(1)} %get-tuple-element.13), channel_id=1, source_target_pairs={{4,0},{8,4},{12,8},{16,12},{20,16},{24,20},{28,24},{32,28},{36,32}... | collective-permute-start | bytes 786440 | tf_op jit(solution)/shard_map/ppermute | solution.py:293
  64.9 0.0 collective-permute-done.4
  64.9 0.1 add_convert_fusion.1
  64.9 21.6 %collective-permute-start.5 = (bf16[4,2,128,128]{3,2,1,0:T(8,128)(2,1)S(1)}, bf16[4,2,128,128]{3,2,1,0:T(8,128)(2,1)S(1)}, u32[]{:S(2)}, u32[]{:S(2)}) collective-permute-start(bf16[4,2,128,128]{3,2,1,0:T(8,128)(2,1)S(1)} %add_convert_fusion.1), channel_id=1, source_target_pairs={{8,0},{12,4},{16,8},{20,12},{24,16},{28,20},{32,24},{36,28},{40,32... | collective-permute-start | bytes 786440 | tf_op jit(solution)/shard_map/ppermute | solution.py:293
  86.5 0.0 collective-permute-done.3
  86.5 3.9 %collective-permute-done.5 = bf16[4,2,128,128]{3,2,1,0:T(8,128)(2,1)S(1)} collective-permute-done((bf16[4,2,128,128]{3,2,1,0:T(8,128)(2,1)S(1)}, bf16[4,2,128,128]{3,2,1,0:T(8,128)(2,1)S(1)}, u32[]{:S(2)}, u32[]{:S(2)}) %collective-permute-start.5) | collective-permute-done | bytes 262176 | tf_op jit(solution)/shard_map/ppermute | solution.py:293
  90.4 0.1 add_convert_fusion
  90.5 0.7 fusion
  (1 shorter events, 0.0 us)
Async XLA Ops:
  2.3 11.0 %all-to-all-start.1 = ((bf16[4,2,128,128]{3,2,1,0:T(8,128)(2,1)}), bf16[4,2,128,128]{3,2,1,0:T(8,128)(2,1)S(1)}, u32[]{:S(2)}, u32[]{:S(2)}) async-start(bf16[4,2,128,128]{3,2,1,0:T(8,128)(2,1)} %pack_2.3), calls=%async_computation.1 | async-start | bytes 524288 | tf_op jit(solution)/shard_map/all_to_all | solution.py:297
  10.5 21.0 %copy-start = (s32[1,4]{1,0:T(1,128)S(1)}, s32[1,4]{1,0:T(1,128)}, u32[]{:S(2)}) copy-start(s32[1,4]{1,0:T(1,128)} %param.11) | copy-start | bytes 52
  13.3 28.8 %all-to-all-start = ((bf16[4,16,128,128]{3,2,1,0:T(8,128)(2,1)}), bf16[4,16,128,128]{3,2,1,0:T(8,128)(2,1)S(1)}, u32[]{:S(2)}, u32[]{:S(2)}) async-start(bf16[4,16,128,128]{3,2,1,0:T(8,128)(2,1)} %pack_2.2), calls=%async_computation | async-start | bytes 4194304 | tf_op jit(solution)/shard_map/all_to_all | solution.py:297
  16.9 12.5 %collective-permute-start.1 = (bf16[4,2,128,128]{3,2,1,0:T(8,128)(2,1)S(1)}, bf16[4,2,128,128]{3,2,1,0:T(8,128)(2,1)S(1)}, u32[]{:S(2)}, u32[]{:S(2)}) collective-permute-start(bf16[4,2,128,128]{3,2,1,0:T(8,128)(2,1)S(1)} %all-to-all-done.1.refs_0_), channel_id=1, source_target_pairs={{0,8},{4,12},{8,16},{12,20},{16,24},{20,28},{24,32},{28,36},{32,40... | collective-permute-start | bytes 786440 | tf_op jit(solution)/shard_map/ppermute | solution.py:293
  22.9 9.8 %collective-permute-start = (bf16[4,2,128,128]{3,2,1,0:T(8,128)(2,1)S(1)}, bf16[4,2,128,128]{3,2,1,0:T(8,128)(2,1)S(1)}, u32[]{:S(2)}, u32[]{:S(2)}) collective-permute-start(bf16[4,2,128,128]{3,2,1,0:T(8,128)(2,1)S(1)} %all-to-all-done.1.refs_0_), channel_id=1, source_target_pairs={{0,4},{4,8},{8,12},{12,16},{16,20},{20,24},{24,28},{28,32},{32,36}... | collective-permute-start | bytes 786440 | tf_op jit(solution)/shard_map/ppermute | solution.py:293
  29.5 9.8 %collective-permute-start.2 = (bf16[4,2,128,128]{3,2,1,0:T(8,128)(2,1)S(1)}, bf16[4,2,128,128]{3,2,1,0:T(8,128)(2,1)S(1)}, u32[]{:S(2)}, u32[]{:S(2)}) collective-permute-start(bf16[4,2,128,128]{3,2,1,0:T(8,128)(2,1)S(1)} %collective-permute-done.1.refs_2_), channel_id=1, source_target_pairs={{0,4},{4,8},{8,12},{12,16},{16,20},{20,24},{24,28},{28,32},{32,36}... | collective-permute-start | bytes 786440 | tf_op jit(solution)/shard_map/ppermute | solution.py:293
  53.1 11.7 %collective-permute-start.4 = (bf16[4,2,128,128]{3,2,1,0:T(8,128)(2,1)S(1)}, bf16[4,2,128,128]{3,2,1,0:T(8,128)(2,1)S(1)}, u32[]{:S(2)}, u32[]{:S(2)}) collective-permute-start(bf16[4,2,128,128]{3,2,1,0:T(8,128)(2,1)S(1)} %get-tuple-element.15), channel_id=1, source_target_pairs={{4,0},{8,4},{12,8},{16,12},{20,16},{24,20},{28,24},{32,28},{36,32}... | collective-permute-start | bytes 786440 | tf_op jit(solution)/shard_map/ppermute | solution.py:293
  57.9 28.6 %collective-permute-start.3 = (bf16[4,2,128,128]{3,2,1,0:T(8,128)(2,1)S(1)}, bf16[4,2,128,128]{3,2,1,0:T(8,128)(2,1)S(1)}, u32[]{:S(2)}, u32[]{:S(2)}) collective-permute-start(bf16[4,2,128,128]{3,2,1,0:T(8,128)(2,1)S(1)} %get-tuple-element.13), channel_id=1, source_target_pairs={{4,0},{8,4},{12,8},{16,12},{20,16},{24,20},{28,24},{32,28},{36,32}... | collective-permute-start | bytes 786440 | tf_op jit(solution)/shard_map/ppermute | solution.py:293
  64.9 25.4 %collective-permute-start.5 = (bf16[4,2,128,128]{3,2,1,0:T(8,128)(2,1)S(1)}, bf16[4,2,128,128]{3,2,1,0:T(8,128)(2,1)S(1)}, u32[]{:S(2)}, u32[]{:S(2)}) collective-permute-start(bf16[4,2,128,128]{3,2,1,0:T(8,128)(2,1)S(1)} %add_convert_fusion.1), channel_id=1, source_target_pairs={{8,0},{12,4},{16,8},{20,12},{24,16},{28,20},{32,24},{36,28},{40,32... | collective-permute-start | bytes 786440 | tf_op jit(solution)/shard_map/ppermute | solution.py:293

commit v2 on v1

--- a/solution.py
+++ b/solution.py
@@ -16,8 +16,7 @@
 TILES = BLOCK // TQ
 LANES = HEADS_PER_GROUP * TQ
 TK = 256
-STEPS = BLOCK // TK
-MOST_STEPS = TILES * PAIRS * STEPS
+MOST_STEPS = 32
 OFFSETS = (3, 2, 1, 0)
 SUMS = HEAD_SIZE + 8
 SCALING = HEAD_SIZE ** (-0.5)
@@ -36,32 +35,38 @@
     return lax.dot_general(a, b, (((1,), (0,)), ((), ())), preferred_element_type=F32)
 
 
-def tile_bias(lo_row, tile, key_start):
-    keys = lax.broadcasted_iota(jnp.int32, (TK, TQ), 0) + key_start
-    last = lax.broadcasted_iota(jnp.int32, (TK, TQ), 1) + ((PAIRS - 1) * BLOCK + tile * TQ)
-    return jnp.where((keys >= lo_row) & (keys <= last), 0.0, MASKED).astype(F32)
+def step_bias(lo_row, meta, n):
+    start, first, last = meta[1, n], meta[2, n], meta[3, n]
+    own = lax.broadcasted_iota(jnp.int32, (1, TQ), 1) + ((PAIRS - 1) * BLOCK + meta[0, n] * TQ)
+    keys = lax.broadcasted_iota(jnp.int32, (TK, TQ), 0) + start
+    seen = (keys >= jnp.maximum(lo_row, first)) & (keys <= jnp.minimum(own, last))
+    return jnp.where(seen, 0.0, MASKED).astype(F32)
 
 
 def list_steps(scalars, meta):
     count = jnp.int32(0)
-    for slot, offset in enumerate(OFFSETS):
-        base = (PAIRS - 1 - offset) * BLOCK
-        for tile in range(TILES):
-            last = (tile * TQ) // TK + 1 if offset == 0 else STEPS
-            first = jnp.minimum(jnp.maximum(scalars[tile] - base, 0) // TK, last)
-            first = jnp.where(scalars[TILES + offset] == 1, first, last)
-
-            def write(i, n, slot=slot, tile=tile, base=base):
-                meta[0, n] = tile
-                meta[1, n] = slot * STEPS + i
-                meta[2, n] = base + i * TK
-                return n + 1
-
-            count = lax.fori_loop(first, last, write, count)
+    for tile in range(TILES):
+        end = (PAIRS - 1) * BLOCK + (tile + 1) * TQ
+        while end > 0:
+            start = max(end - TK, 0)
+            block = start // BLOCK
+            border = (block + 1) * BLOCK
+            first = jnp.where(scalars[TILES + PAIRS - 1 - block] == 1, start, border)
+            last = jnp.int32(end - 1)
+            if border < end:
+                last = jnp.where(scalars[TILES + PAIRS - 2 - block] == 1, last, border - 1)
+            meta[0, count] = tile
+            meta[1, count] = start
+            meta[2, count] = first
+            meta[3, count] = last
+            used = jnp.maximum(first, scalars[tile]) <= last
+            count = count + used.astype(jnp.int32)
+            end = end - TK
     for extra in range(2):
         meta[0, count + extra] = 0
         meta[1, count + extra] = 0
         meta[2, count + extra] = PAIRS * BLOCK
+        meta[3, count + extra] = 0
     return count
 
 
@@ -78,21 +83,42 @@
     lax.fori_loop(0, (count + 1) // 2, body, 0)
 
 
-def rows_of(k):
-    return pl.ds(pl.multiple_of(k * TK, TK), TK)
-
-
-def pack_kernel(*refs):
-    refs, out_ref = refs[:-1], refs[-1]
-    groups = out_ref.shape[0]
-    slot = 0
-    for ref in refs:
-        per_group = ref.shape[1] // HEAD_SIZE // groups
-        for group in range(groups):
-            for h in range(per_group):
-                head = group * per_group + h
-                out_ref[group, slot + h] = ref[:, head * HEAD_SIZE : (head + 1) * HEAD_SIZE]
-        slot += per_group
+def rows_of(start):
+    return pl.ds(pl.multiple_of(start, TQ), TK)
+
+
+def pack_kernel(q_ref, do_ref, x_ref, wide_s, x_s, in_sem, out_sem):
+    width = HEADS_PER_GROUP * HEAD_SIZE
+    wide = [
+        [
+            pltpu.make_async_copy(
+                ref.at[:, pl.ds(group * width, width)], wide_s.at[i, group], in_sem.at[i, group]
+            )
+            for i, ref in enumerate((q_ref, do_ref))
+        ]
+        for group in range(TILES)
+    ]
+    for copy in sum(wide, []):
+        copy.start()
+    out_copies = []
+    for group in range(TILES):
+        for i in range(2):
+            wide[group][i].wait()
+            for h in range(HEADS_PER_GROUP):
+                piece = wide_s[i, group, :, h * HEAD_SIZE : (h + 1) * HEAD_SIZE]
+                x_s[group, i * HEADS_PER_GROUP + h] = piece
+        out_copies.append(pltpu.make_async_copy(x_s.at[group], x_ref.at[group], out_sem.at[group]))
+        out_copies[-1].start()
+    for copy in out_copies:
+        copy.wait()
+
+
+def pack_kv_kernel(place, key_ref, value_ref, *outs):
+    for d, out_ref in enumerate(outs):
+        group = (place[0] + d) % TILES
+        columns = pl.ds(pl.multiple_of(group * HEAD_SIZE, HEAD_SIZE), HEAD_SIZE)
+        out_ref[0] = key_ref[:, columns]
+        out_ref[1] = value_ref[:, columns]
 
 
 def attend_kernel(heads, first_head, first_call, last_call, scalars, x_ref, *refs):
@@ -128,7 +154,8 @@
 
     for slot, kv in enumerate(reversed(kvs)):
         for part in range(TILES):
-            place = slice(slot * BLOCK + part * TQ, slot * BLOCK + (part + 1) * TQ)
+            tokens = (scalars[2 * TILES] + TILES - part) % TILES
+            place = pl.ds(pl.multiple_of(slot * BLOCK + tokens * TQ, TQ), TQ)
             key, value = kv[part, 0], kv[part, 1]
             k_s[place, :] = key
             kt_s[:, place] = key.T
@@ -144,7 +171,7 @@
 
     def weigh(n, buf):
         tile = meta[0, n]
-        bias = tile_bias(lo_ref[tile], tile, meta[2, n])
+        bias = step_bias(lo_ref[tile], meta, n)
         val_t = vt_s[:, rows_of(meta[1, n])]
         m_old = m_s[tile]
         weights, tops = [], []
@@ -225,22 +252,35 @@
     return pl.BlockSpec(memory_space=pltpu.SMEM)
 
 
-def pack(*arrays, steps=1, limit=40):
-    heads = sum(array.shape[1] // HEAD_SIZE // TILES for array in arrays)
-    tokens = arrays[0].shape[0]
+def pack(queries, cotangents):
+    tokens = queries.shape[0]
+    hbm = pl.BlockSpec(memory_space=pltpu.HBM)
+    both = (TILES, 2 * HEADS_PER_GROUP, tokens, HEAD_SIZE)
     return pl.pallas_call(
         pack_kernel,
-        grid=(steps,),
-        in_specs=[
-            pl.BlockSpec((tokens, array.shape[1] // steps), lambda g: (0, g)) for array in arrays
+        in_specs=[hbm] * 2,
+        out_specs=hbm,
+        out_shape=jax.ShapeDtypeStruct(both, BF16),
+        scratch_shapes=[
+            pltpu.VMEM((2, TILES, tokens, HEADS_PER_GROUP * HEAD_SIZE), BF16),
+            pltpu.VMEM(both, BF16),
+            pltpu.SemaphoreType.DMA((2, TILES)),
+            pltpu.SemaphoreType.DMA((TILES,)),
         ],
-        out_specs=pl.BlockSpec(
-            (TILES // steps, heads, tokens, HEAD_SIZE), lambda g: (g, 0, 0, 0)
-        ),
-        out_shape=jax.ShapeDtypeStruct((TILES, heads, tokens, HEAD_SIZE), BF16),
-        compiler_params=pltpu.CompilerParams(vmem_limit_bytes=limit << 20),
-        name="pack_%d" % len(arrays),
-    )(*arrays)
+        compiler_params=pltpu.CompilerParams(vmem_limit_bytes=60 << 20),
+        name="pack",
+    )(queries, cotangents)
+
+
+def pack_kv(place, keys, values):
+    shape = jax.ShapeDtypeStruct((2, keys.shape[0], HEAD_SIZE), BF16)
+    return pl.pallas_call(
+        pack_kv_kernel,
+        in_specs=[smem(), vmem(), vmem()],
+        out_specs=[vmem()] * TILES,
+        out_shape=[shape] * TILES,
+        name="pack_kv",
+    )(place, keys, values)
 
 
 def attend(scalars, x, kvs, lo, first_head, carried):
@@ -276,7 +316,7 @@
             pltpu.VMEM((MOST_STEPS, TK, lanes), BF16),
             pltpu.VMEM((MOST_STEPS, 1, lanes), F32),
             pltpu.VMEM((TILES, TQ, lanes), BF16),
-            pltpu.SMEM((3, MOST_STEPS), jnp.int32),
+            pltpu.SMEM((4, MOST_STEPS), jnp.int32),
             pltpu.SemaphoreType.DMA((2, TILES)),
         ],
         compiler_params=pltpu.CompilerParams(vmem_limit_bytes=(12 + 3 * heads) << 20),
@@ -305,15 +345,22 @@
     return before + begin - (blk - (PAIRS - 1)) * BLOCK
 
 
-def bounds(lo, live):
-    return lo.reshape(TILES, 1, TQ), jnp.concatenate([lo[::TQ], live])
+def bounds(lo, live, place):
+    return lo.reshape(TILES, 1, TQ), jnp.concatenate([lo[::TQ], live, place])
 
 
 def local(queries, key_states, value_projection, output_gradient, doc_ids, pair_live):
     blk = lax.axis_index("ctx")
-    kv0 = exchange(pack(key_states, value_projection, limit=60))
-    x = exchange(pack(queries, output_gradient, steps=4, limit=60))
-    lo, scalars = bounds(window_start(doc_ids, blk), pair_live[0])
+    place = lax.axis_index("tp").astype(jnp.int32).reshape(1)
+    own, *pieces = pack_kv(place, key_states, value_projection)
+    for d, piece in enumerate(pieces, start=1):
+        pieces[d - 1] = lax.ppermute(piece, "tp", [(i, (i + d) % TILES) for i in range(TILES)])
+    queries, output_gradient, own = lax.optimization_barrier((queries, output_gradient, own))
+    x = pack(queries, output_gradient)
+    x, own, *pieces = lax.optimization_barrier((x, own, *pieces))
+    x = exchange(x)
+    kv0 = jnp.stack([own] + pieces)
+    lo, scalars = bounds(window_start(doc_ids, blk), pair_live[0], place)
     kv2 = passed_along(kv0, "ctx", 2)
     kv1 = passed_along(kv0, "ctx", 1)
     kv3 = passed_along(kv2, "ctx", 1)

time: 91.5 us -> 86.8 us (0.949)
  the two profiles are of different devices: /device:TPU:8 before, /device:TPU:97 now
where the time goes in v2:
time: 86.8 us; the launch traced here: 88.4 us
  waiting for transfers between devices  30.5 us (35%)
  starting transfers between devices  28.5 us (33%)
  Pallas kernels  25.3 us (29%)
  local copies, waits for them, and re-layouts  2.37 us (3%)
  other arithmetic  0.87 us (1%)
    ppermute x6, waiting for transfers between devices, passed_along(): lax.ppermute(value, axis, [(source, source + steps) for source in range(i...  26.1 us
    pallas_call x1, Pallas kernels, attend(): pl.pallas_call(functools.partial(attend_kernel, heads, first_head, first_...  21.1 us
    ppermute x6, starting transfers between devices, passed_along(): lax.ppermute(value, axis, [(source, source + steps) for source in range(i...  20.1 us
    ppermute x3, starting transfers between devices, local(): lax.ppermute(piece, 'tp', [(i, (i + d) % TILES) for i in range(TILES)])  4.81 us
    all_to_all x1, waiting for transfers between devices, exchange(): return lax.all_to_all(value, 'tp', split_axis=0, concat_axis=0, tiled=True)  4.33 us
    all_to_all x1, starting transfers between devices, exchange(): return lax.all_to_all(value, 'tp', split_axis=0, concat_axis=0, tiled=True)  3.61 us
    pallas_call x1, Pallas kernels, pack(): pl.pallas_call(pack_kernel, in_specs=[hbm] * 2, out_specs=hbm, out_shape=...  2.51 us
  transfers between devices with their start and end apart: 10, of which 6 were waited for; matrix products, arithmetic and copies ran while one was open for 3% of the time, Pallas kernels for 3%

profile of v2, /device:TPU:97, one launch (start us, length us, event | category | flops | bytes accessed | tf_op | source)
XLA Modules:
  0.0 88.4 jit_solution(11144244746382232800)
XLA Ops:
  0.6 1.7 %pack_kv.1 = (bf16[2,128,128]{2,1,0:T(8,128)(2,1)}, bf16[2,128,128]{2,1,0:T(8,128)(2,1)}, bf16[2,128,128]{2,1,0:T(8,128)(2,1)}, bf16[2,128,128]{2,1,0:T(8,128)(2,1)}) custom-call(s32[1]{0:T(128)} %bitcast.1.place, bf16[128,512]{1,0:T(8,128)(2,1)} %key_ref.1, bf16[128,512]{1,0:T(8,128)(2,1)} %value_ref.1), custom_call_target="tpu_custom_call" | custom-call | tf_op jit(solution)/shard_map/pack_kv/pallas_call | solution.py:277
  2.3 1.2 %collective-permute-start = (bf16[2,128,128]{2,1,0:T(8,128)(2,1)}, bf16[2,128,128]{2,1,0:T(8,128)(2,1)S(1)}, u32[]{:S(2)}, u32[]{:S(2)}) collective-permute-start(bf16[2,128,128]{2,1,0:T(8,128)(2,1)} %get-tuple-element.26), channel_id=1, source_target_pairs={{0,1},{1,2},{2,3},{3,0},{4,5},{5,6},{6,7},{7,4},{8,9},{9,10},{10,1... | collective-permute-start | bytes 196616 | tf_op jit(solution)/shard_map/ppermute | solution.py:357
  3.6 2.5 %collective-permute-start.1 = (bf16[2,128,128]{2,1,0:T(8,128)(2,1)}, bf16[2,128,128]{2,1,0:T(8,128)(2,1)S(1)}, u32[]{:S(2)}, u32[]{:S(2)}) collective-permute-start(bf16[2,128,128]{2,1,0:T(8,128)(2,1)} %get-tuple-element.27), channel_id=1, source_target_pairs={{0,2},{1,3},{2,0},{3,1},{4,6},{5,7},{6,4},{7,5},{8,10},{9,11},{10,... | collective-permute-start | bytes 196616 | tf_op jit(solution)/shard_map/ppermute | solution.py:357
  6.0 1.2 %collective-permute-start.2 = (bf16[2,128,128]{2,1,0:T(8,128)(2,1)}, bf16[2,128,128]{2,1,0:T(8,128)(2,1)S(1)}, u32[]{:S(2)}, u32[]{:S(2)}) collective-permute-start(bf16[2,128,128]{2,1,0:T(8,128)(2,1)} %get-tuple-element.28), channel_id=1, source_target_pairs={{0,3},{1,0},{2,1},{3,2},{4,7},{5,4},{6,5},{7,6},{8,11},{9,8},{10,9... | collective-permute-start | bytes 196616 | tf_op jit(solution)/shard_map/ppermute | solution.py:357
  7.2 2.5 %pack.1 = bf16[4,16,128,128]{3,2,1,0:T(8,128)(2,1)} custom-call(bf16[128,4096]{1,0:T(8,128)(2,1)} %q_ref, bf16[128,4096]{1,0:T(8,128)(2,1)} %do_ref), custom_call_target="tpu_custom_call" | custom-call | tf_op jit(solution)/shard_map/pack/pallas_call | solution.py:259
  9.7 0.0 copy-start
  9.7 0.0 copy-start.1
  9.7 0.0 collective-permute-done
  9.7 0.0 collective-permute-done.1
  9.7 0.1 collective-permute-done.2
  9.9 3.6 %all-to-all-start = ((bf16[4,16,128,128]{3,2,1,0:T(8,128)(2,1)}), bf16[4,16,128,128]{3,2,1,0:T(8,128)(2,1)S(1)}, u32[]{:S(2)}, u32[]{:S(2)}) async-start(bf16[4,16,128,128]{3,2,1,0:T(8,128)(2,1)} %pack.1), calls=%async_computation | async-start | bytes 4194304 | tf_op jit(solution)/shard_map/all_to_all | solution.py:337
  13.5 4.8 %collective-permute-start.4 = (bf16[4,2,128,128]{3,2,1,0:T(8,128)(2,1)S(1)}, bf16[4,2,128,128]{3,2,1,0:T(8,128)(2,1)S(1)}, u32[]{:S(2)}, u32[]{:S(2)}) collective-permute-start(bf16[4,2,128,128]{3,2,1,0:T(8,128)(2,1)S(1)} %pad_maximum_fusion.refs_0_), channel_id=1, source_target_pairs={{0,8},{4,12},{8,16},{12,20},{16,24},{20,28},{24,32},{28,36},{32,40... | collective-permute-start | bytes 786440 | tf_op jit(solution)/shard_map/ppermute | solution.py:333
  18.3 0.8 dynamic_slice.7
  19.1 0.8 dynamic_slice.6
  19.9 0.6 convert_reduce_fusion
  20.4 4.9 %collective-permute-start.3 = (bf16[4,2,128,128]{3,2,1,0:T(8,128)(2,1)S(1)}, bf16[4,2,128,128]{3,2,1,0:T(8,128)(2,1)S(1)}, u32[]{:S(2)}, u32[]{:S(2)}) collective-permute-start(bf16[4,2,128,128]{3,2,1,0:T(8,128)(2,1)S(1)} %pad_maximum_fusion.refs_0_), channel_id=1, source_target_pairs={{0,4},{4,8},{8,12},{12,16},{16,20},{20,24},{24,28},{28,32},{32,36}... | collective-permute-start | bytes 786440 | tf_op jit(solution)/shard_map/ppermute | solution.py:333
  25.4 0.0 collective-permute-done.4.refs_2_
  25.4 4.6 %collective-permute-start.5 = (bf16[4,2,128,128]{3,2,1,0:T(8,128)(2,1)S(1)}, bf16[4,2,128,128]{3,2,1,0:T(8,128)(2,1)S(1)}, u32[]{:S(2)}, u32[]{:S(2)}) collective-permute-start(bf16[4,2,128,128]{3,2,1,0:T(8,128)(2,1)S(1)} %collective-permute-done.4.refs_2_), channel_id=1, source_target_pairs={{0,4},{4,8},{8,12},{12,16},{16,20},{20,24},{24,28},{28,32},{32,36}... | collective-permute-start | bytes 786440 | tf_op jit(solution)/shard_map/ppermute | solution.py:333
  30.0 0.1 slice.11
  30.1 0.1 pad_add_fusion.scalars
  30.2 3.1 %collective-permute-done.5.refs_3_ = bf16[4,2,128,128]{3,2,1,0:T(8,128)(2,1)S(1)} collective-permute-done((bf16[4,2,128,128]{3,2,1,0:T(8,128)(2,1)S(1)}, bf16[4,2,128,128]{3,2,1,0:T(8,128)(2,1)S(1)}, u32[]{:S(2)}, u32[]{:S(2)}) %collective-permute-start.5) | collective-permute-done | bytes 262176 | tf_op jit(solution)/shard_map/ppermute | solution.py:333
  33.3 4.3 %all-to-all-done.x_ref = bf16[4,16,128,128]{3,2,1,0:T(8,128)(2,1)S(1)} async-done(((bf16[4,16,128,128]{3,2,1,0:T(8,128)(2,1)}), bf16[4,16,128,128]{3,2,1,0:T(8,128)(2,1)S(1)}, u32[]{:S(2)}, u32[]{:S(2)}) %all-to-all-start) | async-done | bytes 2097184 | tf_op jit(solution)/shard_map/all_to_all | solution.py:337
  37.6 21.1 %attend_0.1 = (bf16[512,1024]{1,0:T(8,128)(2,1)}, bf16[512,1024]{1,0:T(8,128)(2,1)}, bf16[4,2,128,128]{3,2,1,0:T(8,128)(2,1)S(1)}, bf16[4,2,128,128]{3,2,1,0:T(8...) custom-call(s32[9]{0:T(128)S(1)} %pad_add_fusion.scalars, ...), custom_call_target="tpu_custom_call" | custom-call | flops 16106127360 | bytes 8388608 | tf_op jit(solution)/shard_map/attend_0/pallas_call | solution.py:297
  58.8 1.9 %collective-permute-start.7 = (bf16[4,2,128,128]{3,2,1,0:T(8,128)(2,1)S(1)}, bf16[4,2,128,128]{3,2,1,0:T(8,128)(2,1)S(1)}, u32[]{:S(2)}, u32[]{:S(2)}) collective-permute-start(bf16[4,2,128,128]{3,2,1,0:T(8,128)(2,1)S(1)} %get-tuple-element.39), channel_id=1, source_target_pairs={{4,0},{8,4},{12,8},{16,12},{20,16},{24,20},{28,24},{32,28},{36,32}... | collective-permute-start | bytes 786440 | tf_op jit(solution)/shard_map/ppermute | solution.py:333
  60.7 1.9 %collective-permute-start.6 = (bf16[4,2,128,128]{3,2,1,0:T(8,128)(2,1)S(1)}, bf16[4,2,128,128]{3,2,1,0:T(8,128)(2,1)S(1)}, u32[]{:S(2)}, u32[]{:S(2)}) collective-permute-start(bf16[4,2,128,128]{3,2,1,0:T(8,128)(2,1)S(1)} %get-tuple-element.37), channel_id=1, source_target_pairs={{4,0},{8,4},{12,8},{16,12},{20,16},{24,20},{28,24},{32,28},{36,32}... | collective-permute-start | bytes 786440 | tf_op jit(solution)/shard_map/ppermute | solution.py:333
  62.6 16.3 %collective-permute-done.7 = bf16[4,2,128,128]{3,2,1,0:T(8,128)(2,1)S(1)} collective-permute-done((bf16[4,2,128,128]{3,2,1,0:T(8,128)(2,1)S(1)}, bf16[4,2,128,128]{3,2,1,0:T(8,128)(2,1)S(1)}, u32[]{:S(2)}, u32[]{:S(2)}) %collective-permute-start.7) | collective-permute-done | bytes 262176 | tf_op jit(solution)/shard_map/ppermute | solution.py:333
  78.9 0.1 add_convert_fusion.1
  79.0 1.9 %collective-permute-start.8 = (bf16[4,2,128,128]{3,2,1,0:T(8,128)(2,1)S(1)}, bf16[4,2,128,128]{3,2,1,0:T(8,128)(2,1)S(1)}, u32[]{:S(2)}, u32[]{:S(2)}) collective-permute-start(bf16[4,2,128,128]{3,2,1,0:T(8,128)(2,1)S(1)} %add_convert_fusion.1), channel_id=1, source_target_pairs={{8,0},{12,4},{16,8},{20,12},{24,16},{28,20},{32,24},{36,28},{40,32... | collective-permute-start | bytes 786440 | tf_op jit(solution)/shard_map/ppermute | solution.py:333
  80.9 0.8 collective-permute-done.6
  81.7 5.9 %collective-permute-done.8 = bf16[4,2,128,128]{3,2,1,0:T(8,128)(2,1)S(1)} collective-permute-done((bf16[4,2,128,128]{3,2,1,0:T(8,128)(2,1)S(1)}, bf16[4,2,128,128]{3,2,1,0:T(8,128)(2,1)S(1)}, u32[]{:S(2)}, u32[]{:S(2)}) %collective-permute-start.8) | collective-permute-done | bytes 262176 | tf_op jit(solution)/shard_map/ppermute | solution.py:333
  87.6 0.1 add_convert_fusion
  87.7 0.7 fusion
  (5 shorter events, 0.1 us)
Async XLA Ops:
  2.3 7.4 %collective-permute-start = (bf16[2,128,128]{2,1,0:T(8,128)(2,1)}, bf16[2,128,128]{2,1,0:T(8,128)(2,1)S(1)}, u32[]{:S(2)}, u32[]{:S(2)}) collective-permute-start(bf16[2,128,128]{2,1,0:T(8,128)(2,1)} %get-tuple-element.26), channel_id=1, source_target_pairs={{0,1},{1,2},{2,3},{3,0},{4,5},{5,6},{6,7},{7,4},{8,9},{9,10},{10,1... | collective-permute-start | bytes 196616 | tf_op jit(solution)/shard_map/ppermute | solution.py:357
  3.6 6.2 %collective-permute-start.1 = (bf16[2,128,128]{2,1,0:T(8,128)(2,1)}, bf16[2,128,128]{2,1,0:T(8,128)(2,1)S(1)}, u32[]{:S(2)}, u32[]{:S(2)}) collective-permute-start(bf16[2,128,128]{2,1,0:T(8,128)(2,1)} %get-tuple-element.27), channel_id=1, source_target_pairs={{0,2},{1,3},{2,0},{3,1},{4,6},{5,7},{6,4},{7,5},{8,10},{9,11},{10,... | collective-permute-start | bytes 196616 | tf_op jit(solution)/shard_map/ppermute | solution.py:357
  6.0 3.9 %collective-permute-start.2 = (bf16[2,128,128]{2,1,0:T(8,128)(2,1)}, bf16[2,128,128]{2,1,0:T(8,128)(2,1)S(1)}, u32[]{:S(2)}, u32[]{:S(2)}) collective-permute-start(bf16[2,128,128]{2,1,0:T(8,128)(2,1)} %get-tuple-element.28), channel_id=1, source_target_pairs={{0,3},{1,0},{2,1},{3,2},{4,7},{5,4},{6,5},{7,6},{8,11},{9,8},{10,9... | collective-permute-start | bytes 196616 | tf_op jit(solution)/shard_map/ppermute | solution.py:357
  9.7 3.8 %copy-start = (bf16[2,128,128]{2,1,0:T(8,128)(2,1)S(1)}, bf16[2,128,128]{2,1,0:T(8,128)(2,1)}, u32[]{:S(2)}) copy-start(bf16[2,128,128]{2,1,0:T(8,128)(2,1)} %get-tuple-element.30) | copy-start | bytes 196612
  9.7 20.4 %copy-start.1 = (s32[1,4]{1,0:T(1,128)S(1)}, s32[1,4]{1,0:T(1,128)}, u32[]{:S(2)}) copy-start(s32[1,4]{1,0:T(1,128)} %param.11) | copy-start | bytes 52
  9.9 27.8 %all-to-all-start = ((bf16[4,16,128,128]{3,2,1,0:T(8,128)(2,1)}), bf16[4,16,128,128]{3,2,1,0:T(8,128)(2,1)S(1)}, u32[]{:S(2)}, u32[]{:S(2)}) async-start(bf16[4,16,128,128]{3,2,1,0:T(8,128)(2,1)} %pack.1), calls=%async_computation | async-start | bytes 4194304 | tf_op jit(solution)/shard_map/all_to_all | solution.py:337
  13.5 11.8 %collective-permute-start.4 = (bf16[4,2,128,128]{3,2,1,0:T(8,128)(2,1)S(1)}, bf16[4,2,128,128]{3,2,1,0:T(8,128)(2,1)S(1)}, u32[]{:S(2)}, u32[]{:S(2)}) collective-permute-start(bf16[4,2,128,128]{3,2,1,0:T(8,128)(2,1)S(1)} %pad_maximum_fusion.refs_0_), channel_id=1, source_target_pairs={{0,8},{4,12},{8,16},{12,20},{16,24},{20,28},{24,32},{28,36},{32,40... | collective-permute-start | bytes 786440 | tf_op jit(solution)/shard_map/ppermute | solution.py:333
  20.4 9.8 %collective-permute-start.3 = (bf16[4,2,128,128]{3,2,1,0:T(8,128)(2,1)S(1)}, bf16[4,2,128,128]{3,2,1,0:T(8,128)(2,1)S(1)}, u32[]{:S(2)}, u32[]{:S(2)}) collective-permute-start(bf16[4,2,128,128]{3,2,1,0:T(8,128)(2,1)S(1)} %pad_maximum_fusion.refs_0_), channel_id=1, source_target_pairs={{0,4},{4,8},{8,12},{12,16},{16,20},{20,24},{24,28},{28,32},{32,36}... | collective-permute-start | bytes 786440 | tf_op jit(solution)/shard_map/ppermute | solution.py:333
  25.4 7.9 %collective-permute-start.5 = (bf16[4,2,128,128]{3,2,1,0:T(8,128)(2,1)S(1)}, bf16[4,2,128,128]{3,2,1,0:T(8,128)(2,1)S(1)}, u32[]{:S(2)}, u32[]{:S(2)}) collective-permute-start(bf16[4,2,128,128]{3,2,1,0:T(8,128)(2,1)S(1)} %collective-permute-done.4.refs_2_), channel_id=1, source_target_pairs={{0,4},{4,8},{8,12},{12,16},{16,20},{20,24},{24,28},{28,32},{32,36}... | collective-permute-start | bytes 786440 | tf_op jit(solution)/shard_map/ppermute | solution.py:333
  58.8 20.1 %collective-permute-start.7 = (bf16[4,2,128,128]{3,2,1,0:T(8,128)(2,1)S(1)}, bf16[4,2,128,128]{3,2,1,0:T(8,128)(2,1)S(1)}, u32[]{:S(2)}, u32[]{:S(2)}) collective-permute-start(bf16[4,2,128,128]{3,2,1,0:T(8,128)(2,1)S(1)} %get-tuple-element.39), channel_id=1, source_target_pairs={{4,0},{8,4},{12,8},{16,12},{20,16},{24,20},{28,24},{32,28},{36,32}... | collective-permute-start | bytes 786440 | tf_op jit(solution)/shard_map/ppermute | solution.py:333
  60.7 21.0 %collective-permute-start.6 = (bf16[4,2,128,128]{3,2,1,0:T(8,128)(2,1)S(1)}, bf16[4,2,128,128]{3,2,1,0:T(8,128)(2,1)S(1)}, u32[]{:S(2)}, u32[]{:S(2)}) collective-permute-start(bf16[4,2,128,128]{3,2,1,0:T(8,128)(2,1)S(1)} %get-tuple-element.37), channel_id=1, source_target_pairs={{4,0},{8,4},{12,8},{16,12},{20,16},{24,20},{28,24},{32,28},{36,32}... | collective-permute-start | bytes 786440 | tf_op jit(solution)/shard_map/ppermute | solution.py:333
  79.0 8.6 %collective-permute-start.8 = (bf16[4,2,128,128]{3,2,1,0:T(8,128)(2,1)S(1)}, bf16[4,2,128,128]{3,2,1,0:T(8,128)(2,1)S(1)}, u32[]{:S(2)}, u32[]{:S(2)}) collective-permute-start(bf16[4,2,128,128]{3,2,1,0:T(8,128)(2,1)S(1)} %add_convert_fusion.1), channel_id=1, source_target_pairs={{8,0},{12,4},{16,8},{20,12},{24,16},{28,20},{32,24},{36,28},{40,32... | collective-permute-start | bytes 786440 | tf_op jit(solution)/shard_map/ppermute | solution.py:333

commit v3 on v2

--- a/solution.py
+++ b/solution.py
@@ -188,18 +188,20 @@
         acc_s[tile] = acc_s[tile] * jnp.exp2(m_old - m_new) + dot_nn(val_t, p)
 
     run_steps(count, scores, weigh, buf_a, buf_b)
-    ones = jnp.ones((8, HEAD_SIZE), BF16)
+    ones = jnp.ones((8, 2 * HEAD_SIZE), BF16)
     for tile in range(TILES):
         total = acc_s[tile, HEAD_SIZE : HEAD_SIZE + 1, :]
         m_s[tile] = m_s[tile] + jnp.log2(total)
         inverse = 1.0 / total
+        halves = []
         for h in range(heads):
             out = (acc_s[tile, 0:HEAD_SIZE, columns(h)] * inverse[:, columns(h)]).astype(BF16).T
             att_s[tile, :, columns(h)] = out
             product = out.astype(F32) * x_ref[tile, heads + h].astype(F32)
             high = product.astype(BF16)
             low = (product - high.astype(F32)).astype(BF16)
-            delta_s[tile, :, columns(h)] = (dot_nt(ones, high) + dot_nt(ones, low))[0:1]
+            halves.append(jnp.concatenate([high, low], axis=1))
+        delta_s[tile] = dot_nt(ones, jnp.concatenate(halves, axis=0))[0:1]
         put(tile, att_ref, 0).start()
     if first_call:
         dk_s[...] = jnp.zeros_like(dk_s)

time: 86.8 us -> 84.8 us (0.977)
  the two profiles are of different devices: /device:TPU:97 before, /device:TPU:8 now
where the time goes in v3:
time: 84.8 us; the launch traced here: 83.7 us
  Pallas kernels  31.1 us (37%)
  waiting for transfers between devices  25.6 us (30%)
  starting transfers between devices  23 us (27%)
  local copies, waits for them, and re-layouts  2.37 us (3%)
  other arithmetic  0.86 us (1%)
    pallas_call x1, Pallas kernels, attend(): pl.pallas_call(functools.partial(attend_kernel, heads, first_head, first_...  26.9 us
    ppermute x6, waiting for transfers between devices, passed_along(): lax.ppermute(value, axis, [(source, source + steps) for source in range(i...  22.3 us
    ppermute x6, starting transfers between devices, passed_along(): lax.ppermute(value, axis, [(source, source + steps) for source in range(i...  13.4 us
    ppermute x3, starting transfers between devices, local(): lax.ppermute(piece, 'tp', [(i, (i + d) % TILES) for i in range(TILES)])  5.65 us
    all_to_all x1, starting transfers between devices, exchange(): return lax.all_to_all(value, 'tp', split_axis=0, concat_axis=0, tiled=True)  3.91 us
    all_to_all x1, waiting for transfers between devices, exchange(): return lax.all_to_all(value, 'tp', split_axis=0, concat_axis=0, tiled=True)  2.78 us
    pallas_call x1, Pallas kernels, pack(): pl.pallas_call(pack_kernel, in_specs=[hbm] * 2, out_specs=hbm, out_shape=...  2.51 us
    pallas_call x1, Pallas kernels, pack_kv(): pl.pallas_call(pack_kv_kernel, in_specs=[smem(), vmem(), vmem()], out_spe...  1.71 us
  transfers between devices with their start and end apart: 10, of which 8 were waited for; matrix products, arithmetic and copies ran while one was open for 3% of the time, Pallas kernels for 3%

profile of v3, /device:TPU:8, one launch (start us, length us, event | category | flops | bytes accessed | tf_op | source)
XLA Modules:
  0.0 83.7 jit_solution(3975420332851693004)
XLA Ops:
  0.6 1.7 %pack_kv.1 = (bf16[2,128,128]{2,1,0:T(8,128)(2,1)}, bf16[2,128,128]{2,1,0:T(8,128)(2,1)}, bf16[2,128,128]{2,1,0:T(8,128)(2,1)}, bf16[2,128,128]{2,1,0:T(8,128)(2,1)}) custom-call(s32[1]{0:T(128)} %bitcast.1.place, bf16[128,512]{1,0:T(8,128)(2,1)} %key_ref.1, bf16[128,512]{1,0:T(8,128)(2,1)} %value_ref.1), custom_call_target="tpu_custom_call" | custom-call | tf_op jit(solution)/shard_map/pack_kv/pallas_call | solution.py:279
  2.3 1.5 %collective-permute-start = (bf16[2,128,128]{2,1,0:T(8,128)(2,1)}, bf16[2,128,128]{2,1,0:T(8,128)(2,1)S(1)}, u32[]{:S(2)}, u32[]{:S(2)}) collective-permute-start(bf16[2,128,128]{2,1,0:T(8,128)(2,1)} %get-tuple-element.26), channel_id=1, source_target_pairs={{0,1},{1,2},{2,3},{3,0},{4,5},{5,6},{6,7},{7,4},{8,9},{9,10},{10,1... | collective-permute-start | bytes 196616 | tf_op jit(solution)/shard_map/ppermute | solution.py:359
  3.8 2.7 %collective-permute-start.1 = (bf16[2,128,128]{2,1,0:T(8,128)(2,1)}, bf16[2,128,128]{2,1,0:T(8,128)(2,1)S(1)}, u32[]{:S(2)}, u32[]{:S(2)}) collective-permute-start(bf16[2,128,128]{2,1,0:T(8,128)(2,1)} %get-tuple-element.27), channel_id=1, source_target_pairs={{0,2},{1,3},{2,0},{3,1},{4,6},{5,7},{6,4},{7,5},{8,10},{9,11},{10,... | collective-permute-start | bytes 196616 | tf_op jit(solution)/shard_map/ppermute | solution.py:359
  6.6 1.4 %collective-permute-start.2 = (bf16[2,128,128]{2,1,0:T(8,128)(2,1)}, bf16[2,128,128]{2,1,0:T(8,128)(2,1)S(1)}, u32[]{:S(2)}, u32[]{:S(2)}) collective-permute-start(bf16[2,128,128]{2,1,0:T(8,128)(2,1)} %get-tuple-element.28), channel_id=1, source_target_pairs={{0,3},{1,0},{2,1},{3,2},{4,7},{5,4},{6,5},{7,6},{8,11},{9,8},{10,9... | collective-permute-start | bytes 196616 | tf_op jit(solution)/shard_map/ppermute | solution.py:359
  8.0 2.5 %pack.1 = bf16[4,16,128,128]{3,2,1,0:T(8,128)(2,1)} custom-call(bf16[128,4096]{1,0:T(8,128)(2,1)} %q_ref, bf16[128,4096]{1,0:T(8,128)(2,1)} %do_ref), custom_call_target="tpu_custom_call" | custom-call | tf_op jit(solution)/shard_map/pack/pallas_call | solution.py:261
  10.5 0.0 copy-start
  10.5 0.0 copy-start.1
  10.5 0.0 collective-permute-done
  10.6 0.5 collective-permute-done.2
  11.0 3.9 %all-to-all-start = ((bf16[4,16,128,128]{3,2,1,0:T(8,128)(2,1)}), bf16[4,16,128,128]{3,2,1,0:T(8,128)(2,1)S(1)}, u32[]{:S(2)}, u32[]{:S(2)}) async-start(bf16[4,16,128,128]{3,2,1,0:T(8,128)(2,1)} %pack.1), calls=%async_computation | async-start | bytes 4194304 | tf_op jit(solution)/shard_map/all_to_all | solution.py:339
  15.0 3.8 %collective-permute-start.4 = (bf16[4,2,128,128]{3,2,1,0:T(8,128)(2,1)S(1)}, bf16[4,2,128,128]{3,2,1,0:T(8,128)(2,1)S(1)}, u32[]{:S(2)}, u32[]{:S(2)}) collective-permute-start(bf16[4,2,128,128]{3,2,1,0:T(8,128)(2,1)S(1)} %pad_maximum_fusion.refs_0_), channel_id=1, source_target_pairs={{0,8},{4,12},{8,16},{12,20},{16,24},{20,28},{24,32},{28,36},{32,40... | collective-permute-start | bytes 786440 | tf_op jit(solution)/shard_map/ppermute | solution.py:335
  18.8 0.8 dynamic_slice.7
  19.6 0.8 dynamic_slice.6
  20.4 0.6 convert_reduce_fusion
  21.0 1.9 %collective-permute-start.3 = (bf16[4,2,128,128]{3,2,1,0:T(8,128)(2,1)S(1)}, bf16[4,2,128,128]{3,2,1,0:T(8,128)(2,1)S(1)}, u32[]{:S(2)}, u32[]{:S(2)}) collective-permute-start(bf16[4,2,128,128]{3,2,1,0:T(8,128)(2,1)S(1)} %pad_maximum_fusion.refs_0_), channel_id=1, source_target_pairs={{0,4},{4,8},{8,12},{12,16},{16,20},{20,24},{24,28},{28,32},{32,36}... | collective-permute-start | bytes 786440 | tf_op jit(solution)/shard_map/ppermute | solution.py:335
  22.9 4.6 %collective-permute-done.4.refs_2_ = bf16[4,2,128,128]{3,2,1,0:T(8,128)(2,1)S(1)} collective-permute-done((bf16[4,2,128,128]{3,2,1,0:T(8,128)(2,1)S(1)}, bf16[4,2,128,128]{3,2,1,0:T(8,128)(2,1)S(1)}, u32[]{:S(2)}, u32[]{:S(2)}) %collective-permute-start.4) | collective-permute-done | bytes 262176 | tf_op jit(solution)/shard_map/ppermute | solution.py:335
  27.5 1.9 %collective-permute-start.5 = (bf16[4,2,128,128]{3,2,1,0:T(8,128)(2,1)S(1)}, bf16[4,2,128,128]{3,2,1,0:T(8,128)(2,1)S(1)}, u32[]{:S(2)}, u32[]{:S(2)}) collective-permute-start(bf16[4,2,128,128]{3,2,1,0:T(8,128)(2,1)S(1)} %collective-permute-done.4.refs_2_), channel_id=1, source_target_pairs={{0,4},{4,8},{8,12},{12,16},{16,20},{20,24},{24,28},{28,32},{32,36}... | collective-permute-start | bytes 786440 | tf_op jit(solution)/shard_map/ppermute | solution.py:335
  29.4 0.1 slice.11
  29.5 0.1 pad_add_fusion.scalars
  29.6 1.2 %collective-permute-done.3.refs_1_ = bf16[4,2,128,128]{3,2,1,0:T(8,128)(2,1)S(1)} collective-permute-done((bf16[4,2,128,128]{3,2,1,0:T(8,128)(2,1)S(1)}, bf16[4,2,128,128]{3,2,1,0:T(8,128)(2,1)S(1)}, u32[]{:S(2)}, u32[]{:S(2)}) %collective-permute-start.3) | collective-permute-done | bytes 262176 | tf_op jit(solution)/shard_map/ppermute | solution.py:335
  30.8 6.5 %collective-permute-done.5.refs_3_ = bf16[4,2,128,128]{3,2,1,0:T(8,128)(2,1)S(1)} collective-permute-done((bf16[4,2,128,128]{3,2,1,0:T(8,128)(2,1)S(1)}, bf16[4,2,128,128]{3,2,1,0:T(8,128)(2,1)S(1)}, u32[]{:S(2)}, u32[]{:S(2)}) %collective-permute-start.5) | collective-permute-done | bytes 262176 | tf_op jit(solution)/shard_map/ppermute | solution.py:335
  37.3 2.8 %all-to-all-done.x_ref = bf16[4,16,128,128]{3,2,1,0:T(8,128)(2,1)S(1)} async-done(((bf16[4,16,128,128]{3,2,1,0:T(8,128)(2,1)}), bf16[4,16,128,128]{3,2,1,0:T(8,128)(2,1)S(1)}, u32[]{:S(2)}, u32[]{:S(2)}) %all-to-all-start) | async-done | bytes 2097184 | tf_op jit(solution)/shard_map/all_to_all | solution.py:339
  40.1 26.9 %attend_0.1 = (bf16[512,1024]{1,0:T(8,128)(2,1)}, bf16[512,1024]{1,0:T(8,128)(2,1)}, bf16[4,2,128,128]{3,2,1,0:T(8,128)(2,1)S(1)}, bf16[4,2,128,128]{3,2,1,0:T(8...) custom-call(s32[9]{0:T(128)S(1)} %pad_add_fusion.scalars, ...), custom_call_target="tpu_custom_call" | custom-call | flops 16106127360 | bytes 8388608 | tf_op jit(solution)/shard_map/attend_0/pallas_call | solution.py:299
  66.9 1.9 %collective-permute-start.7 = (bf16[4,2,128,128]{3,2,1,0:T(8,128)(2,1)S(1)}, bf16[4,2,128,128]{3,2,1,0:T(8,128)(2,1)S(1)}, u32[]{:S(2)}, u32[]{:S(2)}) collective-permute-start(bf16[4,2,128,128]{3,2,1,0:T(8,128)(2,1)S(1)} %get-tuple-element.39), channel_id=1, source_target_pairs={{4,0},{8,4},{12,8},{16,12},{20,16},{24,20},{28,24},{32,28},{36,32}... | collective-permute-start | bytes 786440 | tf_op jit(solution)/shard_map/ppermute | solution.py:335
  68.9 1.9 %collective-permute-start.6 = (bf16[4,2,128,128]{3,2,1,0:T(8,128)(2,1)S(1)}, bf16[4,2,128,128]{3,2,1,0:T(8,128)(2,1)S(1)}, u32[]{:S(2)}, u32[]{:S(2)}) collective-permute-start(bf16[4,2,128,128]{3,2,1,0:T(8,128)(2,1)S(1)} %get-tuple-element.37), channel_id=1, source_target_pairs={{4,0},{8,4},{12,8},{16,12},{20,16},{24,20},{28,24},{32,28},{36,32}... | collective-permute-start | bytes 786440 | tf_op jit(solution)/shard_map/ppermute | solution.py:335
  70.8 1.9 %collective-permute-done.7 = bf16[4,2,128,128]{3,2,1,0:T(8,128)(2,1)S(1)} collective-permute-done((bf16[4,2,128,128]{3,2,1,0:T(8,128)(2,1)S(1)}, bf16[4,2,128,128]{3,2,1,0:T(8,128)(2,1)S(1)}, u32[]{:S(2)}, u32[]{:S(2)}) %collective-permute-start.7) | collective-permute-done | bytes 262176 | tf_op jit(solution)/shard_map/ppermute | solution.py:335
  72.7 0.1 add_convert_fusion.1
  72.8 1.9 %collective-permute-start.8 = (bf16[4,2,128,128]{3,2,1,0:T(8,128)(2,1)S(1)}, bf16[4,2,128,128]{3,2,1,0:T(8,128)(2,1)S(1)}, u32[]{:S(2)}, u32[]{:S(2)}) collective-permute-start(bf16[4,2,128,128]{3,2,1,0:T(8,128)(2,1)S(1)} %add_convert_fusion.1), channel_id=1, source_target_pairs={{8,0},{12,4},{16,8},{20,12},{24,16},{28,20},{32,24},{36,28},{40,32... | collective-permute-start | bytes 786440 | tf_op jit(solution)/shard_map/ppermute | solution.py:335
  74.7 0.8 collective-permute-done.6
  75.5 7.3 %collective-permute-done.8 = bf16[4,2,128,128]{3,2,1,0:T(8,128)(2,1)S(1)} collective-permute-done((bf16[4,2,128,128]{3,2,1,0:T(8,128)(2,1)S(1)}, bf16[4,2,128,128]{3,2,1,0:T(8,128)(2,1)S(1)}, u32[]{:S(2)}, u32[]{:S(2)}) %collective-permute-start.8) | collective-permute-done | bytes 262176 | tf_op jit(solution)/shard_map/ppermute | solution.py:335
  82.8 0.1 add_convert_fusion
  83.0 0.7 fusion
  (5 shorter events, 0.1 us)
Async XLA Ops:
  2.3 8.2 %collective-permute-start = (bf16[2,128,128]{2,1,0:T(8,128)(2,1)}, bf16[2,128,128]{2,1,0:T(8,128)(2,1)S(1)}, u32[]{:S(2)}, u32[]{:S(2)}) collective-permute-start(bf16[2,128,128]{2,1,0:T(8,128)(2,1)} %get-tuple-element.26), channel_id=1, source_target_pairs={{0,1},{1,2},{2,3},{3,0},{4,5},{5,6},{6,7},{7,4},{8,9},{9,10},{10,1... | collective-permute-start | bytes 196616 | tf_op jit(solution)/shard_map/ppermute | solution.py:359
  3.8 6.7 %collective-permute-start.1 = (bf16[2,128,128]{2,1,0:T(8,128)(2,1)}, bf16[2,128,128]{2,1,0:T(8,128)(2,1)S(1)}, u32[]{:S(2)}, u32[]{:S(2)}) collective-permute-start(bf16[2,128,128]{2,1,0:T(8,128)(2,1)} %get-tuple-element.27), channel_id=1, source_target_pairs={{0,2},{1,3},{2,0},{3,1},{4,6},{5,7},{6,4},{7,5},{8,10},{9,11},{10,... | collective-permute-start | bytes 196616 | tf_op jit(solution)/shard_map/ppermute | solution.py:359
  6.6 4.5 %collective-permute-start.2 = (bf16[2,128,128]{2,1,0:T(8,128)(2,1)}, bf16[2,128,128]{2,1,0:T(8,128)(2,1)S(1)}, u32[]{:S(2)}, u32[]{:S(2)}) collective-permute-start(bf16[2,128,128]{2,1,0:T(8,128)(2,1)} %get-tuple-element.28), channel_id=1, source_target_pairs={{0,3},{1,0},{2,1},{3,2},{4,7},{5,4},{6,5},{7,6},{8,11},{9,8},{10,9... | collective-permute-start | bytes 196616 | tf_op jit(solution)/shard_map/ppermute | solution.py:359
  10.5 4.4 %copy-start = (bf16[2,128,128]{2,1,0:T(8,128)(2,1)S(1)}, bf16[2,128,128]{2,1,0:T(8,128)(2,1)}, u32[]{:S(2)}) copy-start(bf16[2,128,128]{2,1,0:T(8,128)(2,1)} %get-tuple-element.30) | copy-start | bytes 196612
  10.5 19.0 %copy-start.1 = (s32[1,4]{1,0:T(1,128)S(1)}, s32[1,4]{1,0:T(1,128)}, u32[]{:S(2)}) copy-start(s32[1,4]{1,0:T(1,128)} %param.11) | copy-start | bytes 52
  11.0 29.0 %all-to-all-start = ((bf16[4,16,128,128]{3,2,1,0:T(8,128)(2,1)}), bf16[4,16,128,128]{3,2,1,0:T(8,128)(2,1)S(1)}, u32[]{:S(2)}, u32[]{:S(2)}) async-start(bf16[4,16,128,128]{3,2,1,0:T(8,128)(2,1)} %pack.1), calls=%async_computation | async-start | bytes 4194304 | tf_op jit(solution)/shard_map/all_to_all | solution.py:339
  15.0 12.5 %collective-permute-start.4 = (bf16[4,2,128,128]{3,2,1,0:T(8,128)(2,1)S(1)}, bf16[4,2,128,128]{3,2,1,0:T(8,128)(2,1)S(1)}, u32[]{:S(2)}, u32[]{:S(2)}) collective-permute-start(bf16[4,2,128,128]{3,2,1,0:T(8,128)(2,1)S(1)} %pad_maximum_fusion.refs_0_), channel_id=1, source_target_pairs={{0,8},{4,12},{8,16},{12,20},{16,24},{20,28},{24,32},{28,36},{32,40... | collective-permute-start | bytes 786440 | tf_op jit(solution)/shard_map/ppermute | solution.py:335
  21.0 9.8 %collective-permute-start.3 = (bf16[4,2,128,128]{3,2,1,0:T(8,128)(2,1)S(1)}, bf16[4,2,128,128]{3,2,1,0:T(8,128)(2,1)S(1)}, u32[]{:S(2)}, u32[]{:S(2)}) collective-permute-start(bf16[4,2,128,128]{3,2,1,0:T(8,128)(2,1)S(1)} %pad_maximum_fusion.refs_0_), channel_id=1, source_target_pairs={{0,4},{4,8},{8,12},{12,16},{16,20},{20,24},{24,28},{28,32},{32,36}... | collective-permute-start | bytes 786440 | tf_op jit(solution)/shard_map/ppermute | solution.py:335
  27.5 9.8 %collective-permute-start.5 = (bf16[4,2,128,128]{3,2,1,0:T(8,128)(2,1)S(1)}, bf16[4,2,128,128]{3,2,1,0:T(8,128)(2,1)S(1)}, u32[]{:S(2)}, u32[]{:S(2)}) collective-permute-start(bf16[4,2,128,128]{3,2,1,0:T(8,128)(2,1)S(1)} %collective-permute-done.4.refs_2_), channel_id=1, source_target_pairs={{0,4},{4,8},{8,12},{12,16},{16,20},{20,24},{24,28},{28,32},{32,36}... | collective-permute-start | bytes 786440 | tf_op jit(solution)/shard_map/ppermute | solution.py:335
  66.9 5.8 %collective-permute-start.7 = (bf16[4,2,128,128]{3,2,1,0:T(8,128)(2,1)S(1)}, bf16[4,2,128,128]{3,2,1,0:T(8,128)(2,1)S(1)}, u32[]{:S(2)}, u32[]{:S(2)}) collective-permute-start(bf16[4,2,128,128]{3,2,1,0:T(8,128)(2,1)S(1)} %get-tuple-element.39), channel_id=1, source_target_pairs={{4,0},{8,4},{12,8},{16,12},{20,16},{24,20},{28,24},{32,28},{36,32}... | collective-permute-start | bytes 786440 | tf_op jit(solution)/shard_map/ppermute | solution.py:335
  68.9 6.7 %collective-permute-start.6 = (bf16[4,2,128,128]{3,2,1,0:T(8,128)(2,1)S(1)}, bf16[4,2,128,128]{3,2,1,0:T(8,128)(2,1)S(1)}, u32[]{:S(2)}, u32[]{:S(2)}) collective-permute-start(bf16[4,2,128,128]{3,2,1,0:T(8,128)(2,1)S(1)} %get-tuple-element.37), channel_id=1, source_target_pairs={{4,0},{8,4},{12,8},{16,12},{20,16},{24,20},{28,24},{32,28},{36,32}... | collective-permute-start | bytes 786440 | tf_op jit(solution)/shard_map/ppermute | solution.py:335
  72.8 10.0 %collective-permute-start.8 = (bf16[4,2,128,128]{3,2,1,0:T(8,128)(2,1)S(1)}, bf16[4,2,128,128]{3,2,1,0:T(8,128)(2,1)S(1)}, u32[]{:S(2)}, u32[]{:S(2)}) collective-permute-start(bf16[4,2,128,128]{3,2,1,0:T(8,128)(2,1)S(1)} %add_convert_fusion.1), channel_id=1, source_target_pairs={{8,0},{12,4},{16,8},{20,12},{24,16},{28,20},{32,24},{36,28},{40,32... | collective-permute-start | bytes 786440 | tf_op jit(solution)/shard_map/ppermute | solution.py:335
